TPU v7x, 128 devices: a whole 4x4x4 slice. The times are simulated.
128 devices in a mesh: section: 4 (over z), ctx: 32 (over y, x, core).
Axes of the slice: x: 4, y: 4, z: 4, core: 2. Of those that a mesh axis runs over, the one named last changes fastest.
Arguments:
- text_embeds: bfloat16 [4096, 8192], P('ctx'), may hold values from -6 to 6
- patches: bfloat16 [256, 5120], P('ctx'), may hold values from -6 to 6
- vis_gain: float32 [5120], replicated, may hold values from 0.25 to 1.75
- w_merge: bfloat16 [5120, 8192], P(None, 'ctx'), may hold values from -0.078125 to 0.078125
- frame_count: int32 [32], replicated, may hold values from 0 to 2, as said below
- frame_offset: int32 [64], replicated, may hold values from 0 to 4092, as said below
- doc_ids: int32 [4096], replicated, may hold values from 0 to 7, never falling along the last dimension, each value on 1 to 2048 neighbouring positions
- norm_gain: float32 [4, 8192], P('section'), may hold values from 0.25 to 1.75
- w_key: bfloat16 [4, 8192, 512], P('section', 'ctx'), may hold values from -0.0625 to 0.0625
- w_value: bfloat16 [4, 8192, 512], P('section', 'ctx'), may hold values from -0.0625 to 0.0625
- queries: bfloat16 [4, 4096, 8192], P('section', 'ctx'), may hold values from -576 to 576
Outputs:
- layer_out: bfloat16 [4, 4096, 8192], P('section', 'ctx')
Inputs may be any that keep to these rules, and one draw needn't show every extreme that they name: `frame_count`: some index of ctx uses all 2 slots. `frame_offset`: distinct multiples of 4; at most 4 of them lie among the 128 positions of one index of ctx, and some index holds exactly that many.
All inputs are finite; a program needn't handle non-finite values.
Results may differ from a plain program's by a relative error of at most 0.0071.
The roundings to bfloat16 on the way count: a program that leaves them out, or rounds other values in their place, can miss the bound.
Values may be sent and summed in bfloat16 or wider, within the bound.
A program may use at most 320 MiB of HBM per device.

v0:
```python
import math

import jax
import jax.numpy as jnp
from jax import lax
from jax.sharding import PartitionSpec as P

QH = 64


def passed_along(block, axis, distance):
    devices = range(lax.axis_size(axis))
    route = [(i - distance, i) for i in devices if i - distance in devices]
    return lax.ppermute(block, axis, route)


def rms_norm(values, gain):
    wide = values.astype(jnp.float32)
    scale = lax.rsqrt(jnp.mean(wide * wide, axis=-1, keepdims=True) + 1e-06)
    return (wide * scale * gain).astype(jnp.bfloat16)


def shards(
    text_embeds,
    patches,
    vis_gain,
    w_merge,
    frame_count,
    frame_offset,
    doc_ids,
    norm_gain,
    w_key,
    w_value,
    queries,
):
    ctx_count = lax.axis_size("ctx")
    ctx_index = lax.axis_index("ctx")
    section_index = lax.axis_index("section")
    section_count = lax.axis_size("section")
    tok_count = text_embeds.shape[0]
    width = text_embeds.shape[1]
    slots = frame_offset.shape[0]
    slot_dev = slots // ctx_count
    column_part = jnp.dot(
        rms_norm(lax.all_gather(patches, "ctx", axis=0, tiled=True), vis_gain),
        w_merge,
        preferred_element_type=jnp.float32,
    ).astype(jnp.bfloat16)
    vision_rows = column_part.shape[0]
    frame_tok = vision_rows // slots
    row_index = jnp.arange(vision_rows, dtype=jnp.int32)
    slot = row_index // frame_tok
    owner = slot // slot_dev
    used = slot % slot_dev < frame_count[owner]
    dest = frame_offset[slot] + row_index % frame_tok
    own_pos = ctx_index * tok_count + jnp.arange(tok_count, dtype=jnp.int32)
    own_match = (dest[None, :] == own_pos[:, None]) & used[None, :]
    covered = jnp.any(own_match, axis=1)
    full_rows = lax.all_gather(column_part, "ctx", axis=1, tiled=True)
    placed = jnp.dot(
        own_match.astype(jnp.bfloat16), full_rows, preferred_element_type=jnp.float32
    ).astype(jnp.bfloat16)
    joined = jnp.where(covered[:, None], placed, text_embeds)
    kv_width = w_key.shape[2]
    query_dim = queries.shape[2]
    qdoc = lax.dynamic_slice_in_dim(doc_ids, ctx_index * tok_count, tok_count, 0)
    normed = rms_norm(joined, norm_gain[0])
    pieces = (
        lax.all_gather(w_key[0], "ctx", axis=0, tiled=True),
        lax.all_gather(w_value[0], "ctx", axis=0, tiled=True),
    )
    key_sum = jnp.dot(normed, pieces[0], preferred_element_type=jnp.float32)
    value_sum = jnp.dot(normed, pieces[1], preferred_element_type=jnp.float32)
    keys = key_sum.astype(jnp.bfloat16)
    values = value_sum.astype(jnp.bfloat16)
    size_head = query_dim // QH
    kv_count = kv_width // size_head
    groups = QH // kv_count
    query = queries[0].reshape(tok_count, kv_count, groups, size_head)
    scale = 1.0 / math.sqrt(size_head)
    all_keys, all_values = (
        lax.all_gather(keys, "ctx", axis=0, tiled=True),
        lax.all_gather(values, "ctx", axis=0, tiled=True),
    )
    pieces = (all_keys, all_values)
    top = jnp.full((tok_count, kv_count, groups), -1e30, jnp.float32)
    total = jnp.zeros((tok_count, kv_count, groups), jnp.float32)
    accum = jnp.zeros((tok_count, kv_count, groups, size_head), jnp.float32)
    count = pieces[0].shape[0]
    step = math.gcd(count, 512)
    for block in range(count // step):
        key_block = pieces[0][block * step : (block + 1) * step].reshape(step, kv_count, size_head)
        value_block = pieces[1][block * step : (block + 1) * step].reshape(
            step, kv_count, size_head
        )
        kpos = 0 + block * step + jnp.arange(step, dtype=jnp.int32)
        kdoc = lax.dynamic_slice_in_dim(doc_ids, 0 + block * step, step, 0)
        allowed = (kpos[None, :] <= own_pos[:, None]) & (kdoc[None, :] == qdoc[:, None])
        scores = (
            jnp.einsum("tkgd,nkd->tkgn", query, key_block, preferred_element_type=jnp.float32)
            * scale
        )
        scores = jnp.where(allowed[:, None, None, :], scores, -1e30)
        new_top = jnp.maximum(top, jnp.max(scores, axis=-1))
        shrink = jnp.exp(top - new_top)
        expo = jnp.exp(scores - new_top[..., None]) * allowed[:, None, None, :]
        total = total * shrink + jnp.sum(expo, axis=-1)
        accum = accum * shrink[..., None] + jnp.einsum(
            "tkgn,nkd->tkgd", expo, value_block.astype(jnp.float32)
        )
        top = new_top
    top, total, accum = (top, total, accum)
    mixed = (accum / total[..., None]).reshape(tok_count, width)
    carried = joined
    result = jnp.zeros_like(joined)
    for turn in range(section_count):
        if turn > 0:
            carried = passed_along(carried, "section", 1)
        updated = (carried.astype(jnp.float32) + mixed).astype(jnp.bfloat16)
        carried = jnp.where(section_index == turn, updated, carried)
        result = jnp.where(section_index == turn, updated, result)
    return result.reshape(1, tok_count, width)


def solution(mesh):
    return jax.shard_map(
        shards,
        mesh=mesh,
        in_specs=(
            P("ctx", None),
            P("ctx", None),
            P(),
            P(None, "ctx"),
            P(),
            P(),
            P(),
            P("section", None),
            P("section", "ctx", None),
            P("section", "ctx", None),
            P("section", "ctx", None),
        ),
        out_specs=P("section", "ctx", None),
        check_vma=False,
    )
```

profile of v0, /device:TPU:96, one launch (start us, length us, event | category | flops | bytes accessed | tf_op | source)
XLA Modules:
  0.0 748.4 jit_solution(11397460654039410464)
XLA Ops:
  7.3 48.0 %all-gather.9.cloned.1.call-done = bf16[256,5120]{1,0:T(8,128)(2,1)} async-done(((bf16[8,5120]{1,0:T(8,128)(2,1)}), bf16[256,5120]{1,0:T(8,128)(2,1)}) %all-gather.9.cloned.1.call-update) | async-done | bytes 2621456 | tf_op jit(solution)/shard_map/all_gather | solution.py:45
  73.7 15.7 %fusion.130 = pred[256]{0:T(512)(128)(4,1)S(1)} fusion(pred[256]{0:T(512)(128)(4,1)S(1)} %compare_reduce_fusion, pred[256]{0:T(512)(128)(4,1)S(1)} %compare_reduce_fusion.1, pred[256]{0:T(512)(128)(4,1)S(1)} %compare_reduce_fusion.2, pred[256]{0:T(512)(128)(4,1)S(1)} %compare_reduce_fusion.3, pred[256]{0:T(512)(128)(4,1)S(1)} %compare_reduce_fusion.4, ...), kind=kLoop, calls=%fused_computation.233 | loop fusion | flops 11520 | bytes 7780 | tf_op jit(solution)/shard_map/lt | solution.py:54
  89.5 20.2 %all-gather.11.cloned.1.call-done = bf16[256,8192]{1,0:T(8,128)(2,1)} async-done(((bf16[256,256]{1,0:T(8,128)(2,1)}), bf16[256,8192]{1,0:T(8,128)(2,1)}) %all-gather.11.cloned.1.call-update) | async-done | bytes 4194320 | tf_op jit(solution)/shard_map/all_gather | solution.py:59
  113.8 50.6 %all-gather.17.cloned.1.call-done = bf16[1,8192,512]{2,1,0:T(8,128)(2,1)} async-done(((bf16[1,256,512]{2,1,0:T(8,128)(2,1)}), bf16[1,8192,512]{2,1,0:T(8,128)(2,1)}) %all-gather.17.cloned.1.call-update) | async-done | bytes 8388624 | tf_op jit(solution)/shard_map/all_gather | solution.py:69
  169.7 49.1 %all-gather.19.cloned.1.call-done = bf16[1,8192,512]{2,1,0:T(8,128)(2,1)} async-done(((bf16[1,256,512]{2,1,0:T(8,128)(2,1)}), bf16[1,8192,512]{2,1,0:T(8,128)(2,1)}) %all-gather.19.cloned.1.call-update) | async-done | bytes 8388624 | tf_op jit(solution)/shard_map/all_gather | solution.py:70
  229.8 36.8 %all-gather.13.cloned.1.call-done = bf16[4096,512]{1,0:T(8,128)(2,1)} async-done(((bf16[128,512]{1,0:T(8,128)(2,1)}), bf16[4096,512]{1,0:T(8,128)(2,1)}) %all-gather.13.cloned.1.call-update) | async-done | bytes 4194320 | tf_op jit(solution)/shard_map/all_gather | solution.py:82
  271.8 42.4 %all-gather.15.cloned.1.call-done = bf16[4096,512]{1,0:T(8,128)(2,1)} async-done(((bf16[128,512]{1,0:T(8,128)(2,1)}), bf16[4096,512]{1,0:T(8,128)(2,1)}) %all-gather.15.cloned.1.call-update) | async-done | bytes 4194320 | tf_op jit(solution)/shard_map/all_gather | solution.py:83
  352.6 8.1 %fusion.5 = (f32[128,4,16]{0,2,1:T(8,128)S(1)}, f32[4,512,128,16]{2,1,3,0:T(8,128)}) fusion(pred[128,512]{0,1:T(8,128)(4,1)S(1)} %get-tuple-element.62, bf16[128,4,16,128]{3,2,1,0:T(8,128)(2,1)S(1)} %bitcast.231, bf16[512,4,128,1]{2,1,0,3:T(4,128)(2,1)S(1)} %bitcast.246), kind=kOutput, calls=%fused_computation.22 | convolution fusion | flops 1086316544 | bytes 19496960 | tf_op jit(solution)/shard_map/tkgd,nkd->tkgn/dot_general | solution.py:100
  368.4 7.7 %fusion.3 = (f32[128,4,16]{0,2,1:T(8,128)S(1)}, f32[4,512,128,16]{2,1,3,0:T(8,128)}) fusion(pred[128,512]{0,1:T(8,128)(4,1)S(1)} %get-tuple-element.66, bf16[128,4,16,128]{3,2,1,0:T(8,128)(2,1)S(1)} %bitcast.233, bf16[512,4,128,1]{2,1,0,3:T(4,128)(2,1)S(1)} %bitcast.243), kind=kOutput, calls=%fused_computation.20 | convolution fusion | flops 1086316544 | bytes 19496960 | tf_op jit(solution)/shard_map/tkgd,nkd->tkgn/dot_general | solution.py:100
  406.5 12.2 %fusion.9 = f32[4,128,128,16]{2,1,3,0:T(8,128)} fusion(bf16[512,4,128,1]{0,2,3,1:T(8,128)(2,1)S(1)} %bitcast.255, f32[4,512,128,16]{2,1,3,0:T(8,128)} %get-tuple-element.125, f32[128,512]{0,1:T(8,128)S(1)} %copy-done.19, f32[128,4,16]{0,2,1:T(8,128)S(1)} %get-tuple-element.37, pred[128,512]{0,1:T(8,128)(4,1)S(1)} %copy-done.11), kind=kOutput, calls=%fused_computation.26 | convolution fusion | flops 1090519040 | bytes 21856256 | tf_op jit(solution)/shard_map/tkgn,nkd->tkgd/dot_general | solution.py:108
  418.7 14.0 %fusion.8 = (f32[128,4,16]{0,2,1:T(8,128)S(1)}, f32[128,4,16]{0,2,1:T(8,128)S(1)}) fusion(f32[4,512,128,16]{2,1,3,0:T(8,128)} %get-tuple-element.125, f32[128,512]{0,1:T(8,128)S(1)} %copy-done.19, f32[128,4,16]{0,2,1:T(8,128)S(1)} %get-tuple-element.37, pred[128,512]{0,1:T(8,128)(4,1)S(1)} %copy-done.11, f32[128,512]{0,1:T(8,128)S(1)} %copy-done.18, ...), kind=kLoop, calls=%fused_computation.25 | loop fusion | flops 41926656 | bytes 34340864 | tf_op jit(solution)/shard_map/reduce_sum | solution.py:107
  432.7 12.3 %fusion.11 = f32[4,128,128,16]{2,1,3,0:T(8,128)} fusion(bf16[512,4,128,1]{0,2,3,1:T(8,128)(2,1)S(1)} %bitcast.254, f32[4,512,128,16]{2,1,3,0:T(8,128)} %get-tuple-element.123, f32[128,512]{0,1:T(8,128)S(1)} %copy-done.18, f32[128,4,16]{0,2,1:T(8,128)S(1)} %get-tuple-element.19, pred[128,512]{0,1:T(8,128)(4,1)S(1)} %copy-done.10), kind=kOutput, calls=%fused_computation.28 | convolution fusion | flops 1090519040 | bytes 21856256 | tf_op jit(solution)/shard_map/tkgn,nkd->tkgd/dot_general | solution.py:108
  445.0 12.3 %fusion.19 = f32[4,128,128,16]{2,1,3,0:T(8,128)} fusion(bf16[512,4,128,1]{0,2,3,1:T(8,128)(2,1)S(1)} %bitcast.253, f32[4,512,128,16]{2,1,3,0:T(8,128)} %get-tuple-element.115, f32[128,512]{0,1:T(8,128)S(1)} %copy-done.17, f32[128,4,16]{0,2,1:T(8,128)S(1)} %get-tuple-element.15, pred[128,512]{0,1:T(8,128)(4,1)S(1)} %get-tuple-element.62), kind=kOutput, calls=%fused_computation.36 | convolution fusion | flops 1090519040 | bytes 21856256 | tf_op jit(solution)/shard_map/tkgn,nkd->tkgd/dot_general | solution.py:108
  457.3 14.2 %fusion.16 = (f32[128,4,16]{0,2,1:T(8,128)S(1)}, f32[128,4,16]{0,2,1:T(8,128)S(1)}) fusion(f32[4,512,128,16]{2,1,3,0:T(8,128)} %get-tuple-element.117, f32[128,512]{0,1:T(8,128)S(1)} %copy-done.16, f32[128,4,16]{0,2,1:T(8,128)S(1)} %get-tuple-element.16, pred[128,512]{0,1:T(8,128)(4,1)S(1)} %get-tuple-element.64, f32[128,512]{0,1:T(8,128)S(1)} %copy-done.17, ...), kind=kLoop, calls=%fused_computation.33 | loop fusion | flops 41926656 | bytes 34340864 | tf_op jit(solution)/shard_map/reduce_sum | solution.py:107
  471.5 12.2 %fusion.17 = f32[4,128,128,16]{2,1,3,0:T(8,128)} fusion(bf16[512,4,128,1]{0,2,3,1:T(8,128)(2,1)S(1)} %bitcast.252, f32[4,512,128,16]{2,1,3,0:T(8,128)} %get-tuple-element.117, f32[128,512]{0,1:T(8,128)S(1)} %copy-done.16, f32[128,4,16]{0,2,1:T(8,128)S(1)} %get-tuple-element.16, pred[128,512]{0,1:T(8,128)(4,1)S(1)} %get-tuple-element.64), kind=kOutput, calls=%fused_computation.34 | convolution fusion | flops 1090519040 | bytes 21856256 | tf_op jit(solution)/shard_map/tkgn,nkd->tkgd/dot_general | solution.py:108
  483.7 12.2 %fusion.15 = f32[4,128,128,16]{2,1,3,0:T(8,128)} fusion(bf16[512,4,128,1]{0,2,3,1:T(8,128)(2,1)S(1)} %bitcast.251, f32[4,512,128,16]{2,1,3,0:T(8,128)} %get-tuple-element.119, f32[128,512]{0,1:T(8,128)S(1)} %copy-done.15, f32[128,4,16]{0,2,1:T(8,128)S(1)} %get-tuple-element.17, pred[128,512]{0,1:T(8,128)(4,1)S(1)} %get-tuple-element.66), kind=kOutput, calls=%fused_computation.32 | convolution fusion | flops 1090519040 | bytes 21856256 | tf_op jit(solution)/shard_map/tkgn,nkd->tkgd/dot_general | solution.py:108
  495.9 13.9 %fusion.12 = (f32[128,4,16]{0,2,1:T(8,128)S(1)}, f32[128,4,16]{0,2,1:T(8,128)S(1)}) fusion(f32[4,512,128,16]{2,1,3,0:T(8,128)} %get-tuple-element.121, f32[128,512]{0,1:T(8,128)S(1)} %copy-done.14, f32[128,4,16]{0,2,1:T(8,128)S(1)} %get-tuple-element.18, pred[128,512]{0,1:T(8,128)(4,1)S(1)} %get-tuple-element.68, f32[128,512]{0,1:T(8,128)S(1)} %copy-done.15, ...), kind=kLoop, calls=%fused_computation.29 | loop fusion | flops 41926656 | bytes 34340864 | tf_op jit(solution)/shard_map/reduce_sum | solution.py:107
  509.9 12.3 %fusion.13 = f32[4,128,128,16]{2,1,3,0:T(8,128)} fusion(bf16[512,4,128,1]{0,2,3,1:T(8,128)(2,1)S(1)} %bitcast.250, f32[4,512,128,16]{2,1,3,0:T(8,128)} %get-tuple-element.121, f32[128,512]{0,1:T(8,128)S(1)} %copy-done.14, f32[128,4,16]{0,2,1:T(8,128)S(1)} %get-tuple-element.18, pred[128,512]{0,1:T(8,128)(4,1)S(1)} %get-tuple-element.68), kind=kOutput, calls=%fused_computation.30 | convolution fusion | flops 1090519040 | bytes 21856256 | tf_op jit(solution)/shard_map/tkgn,nkd->tkgd/dot_general | solution.py:108
  522.2 12.2 %fusion.21 = f32[4,128,128,16]{2,1,3,0:T(8,128)} fusion(bf16[512,4,128,1]{0,2,3,1:T(8,128)(2,1)S(1)} %bitcast.249, f32[4,512,128,16]{2,1,3,0:T(8,128)} %get-tuple-element.113, f32[128,512]{0,1:T(8,128)S(1)} %copy-done.13, f32[128,4,16]{0,2,1:T(8,128)S(1)} %get-tuple-element.14, pred[128,512]{0,1:T(8,128)(4,1)S(1)} %get-tuple-element.75), kind=kOutput, calls=%fused_computation.38 | convolution fusion | flops 1090519040 | bytes 21856256 | tf_op jit(solution)/shard_map/tkgn,nkd->tkgd/dot_general | solution.py:108
  534.4 10.8 %fusion.20 = (f32[128,4,16]{0,2,1:T(8,128)S(1)}, f32[128,4,16]{0,2,1:T(8,128)S(1)}) fusion(f32[4,512,128,16]{2,1,3,0:T(8,128)} %get-tuple-element.113, f32[128,512]{0,1:T(8,128)S(1)} %copy-done.13, f32[128,4,16]{0,2,1:T(8,128)S(1)} %get-tuple-element.14, pred[128,512]{0,1:T(8,128)(4,1)S(1)} %get-tuple-element.75, f32[128,512]{0,1:T(8,128)S(1)} %copy-done.12, ...), kind=kLoop, calls=%fused_computation.37 | loop fusion | flops 41926656 | bytes 34340864 | tf_op jit(solution)/shard_map/reduce_sum | solution.py:107
  545.3 19.8 %fusion.76 = f32[128,4,16,128]{0,3,2,1:T(8,128)} fusion(f32[4,128,128,16]{2,1,3,0:T(8,128)} %fusion.21, f32[4,128,128,16]{2,1,3,0:T(8,128)} %fusion.19, f32[4,128,128,16]{2,1,3,0:T(8,128)} %fusion.17, f32[4,128,128,16]{2,1,3,0:T(8,128)} %fusion.15, f32[4,128,128,16]{2,1,3,0:T(8,128)} %fusion.13, f32[4,128,128,16]{2,1,3,0:T(8,128)} %fusion.11, ...), kind=kOutput, calls=%fused_computation.100 | convolution fusion | flops 1107296256 | bytes 51511296 | tf_op jit(solution)/shard_map/tkgn,nkd->tkgd/dot_general | solution.py:108
  577.7 48.7 %collective-permute-done = bf16[128,8192]{1,0:T(8,128)(2,1)} collective-permute-done((bf16[128,8192]{1,0:T(8,128)(2,1)}, bf16[128,8192]{1,0:T(8,128)(2,1)}, u32[]{:S(2)}, u32[]{:S(2)}) %collective-permute-start) | collective-permute-done | bytes 2097184 | tf_op jit(solution)/shard_map/ppermute | solution.py:14
  633.3 47.9 %collective-permute-done.1 = bf16[128,8192]{1,0:T(8,128)(2,1)} collective-permute-done((bf16[128,8192]{1,0:T(8,128)(2,1)}, bf16[128,8192]{1,0:T(8,128)(2,1)}, u32[]{:S(2)}, u32[]{:S(2)}) %collective-permute-start.1) | collective-permute-done | bytes 2097184 | tf_op jit(solution)/shard_map/ppermute | solution.py:14
  687.9 47.0 %collective-permute-done.2 = bf16[128,8192]{1,0:T(8,128)(2,1)} collective-permute-done((bf16[128,8192]{1,0:T(8,128)(2,1)}, bf16[128,8192]{1,0:T(8,128)(2,1)}, u32[]{:S(2)}, u32[]{:S(2)}) %collective-permute-start.2) | collective-permute-done | bytes 2097184 | tf_op jit(solution)/shard_map/ppermute | solution.py:14
  (158 shorter events, 153.7 us)
Async XLA Ops:
  6.5 51.1 %copy-start = (bf16[5120,256]{1,0:T(8,128)(2,1)S(1)}, bf16[5120,256]{1,0:T(8,128)(2,1)}, u32[]{:S(2)}) copy-start(bf16[5120,256]{1,0:T(8,128)(2,1)} %param.14) | copy-start | bytes 7864324
  6.5 157.8 %copy-start.29 = (f32[1,8192]{1,0:T(1,128)S(1)}, f32[1,8192]{1,0:T(1,128)}, u32[]{:S(2)}) copy-start(f32[1,8192]{1,0:T(1,128)} %param.18) | copy-start | bytes 98308
  6.5 48.8 %all-gather.9.cloned.1.call-start = ((), (), s32[]{:S(2)}) async-start(), calls=%async_computation | async-start | bytes 2703360 | tf_op jit(solution)/shard_map/all_gather | solution.py:45
  7.3 102.5 %all-gather.11.cloned.1.call-start = ((), (), s32[]{:S(2)}) async-start(), calls=%async_computation.1 | async-start | bytes 4325376 | tf_op jit(solution)/shard_map/all_gather | solution.py:59
  61.0 103.4 %all-gather.17.cloned.1.call-start = ((), (), s32[]{:S(2)}) async-start(), calls=%async_computation.4 | async-start | bytes 8650752 | tf_op jit(solution)/shard_map/all_gather | solution.py:69
  61.7 157.2 %all-gather.19.cloned.1.call-start = ((), (), s32[]{:S(2)}) async-start(), calls=%async_computation.5 | async-start | bytes 8650752 | tf_op jit(solution)/shard_map/all_gather | solution.py:70
  62.3 204.3 %all-gather.13.cloned.1.call-start = ((), (), s32[]{:S(2)}) async-start(), calls=%async_computation.2 | async-start | bytes 4325376 | tf_op jit(solution)/shard_map/all_gather | solution.py:82
  113.8 110.5 %copy-start.3 = (bf16[128,8192]{1,0:T(8,128)(2,1)}, bf16[128,8192]{1,0:T(8,128)(2,1)S(1)}, u32[]{:S(2)}) copy-start(bf16[128,8192]{1,0:T(8,128)(2,1)S(1)} %get-tuple-element.109) | copy-start | bytes 6291460
  169.7 56.8 %copy-start.28 = (s32[4096]{0:T(1024)S(1)}, s32[4096]{0:T(1024)}, u32[]{:S(2)}) copy-start(s32[4096]{0:T(1024)} %param.17) | copy-start | bytes 49156
  169.7 144.4 %all-gather.15.cloned.1.call-start = ((), (), s32[]{:S(2)}) async-start(), calls=%async_computation.3 | async-start | bytes 4325376 | tf_op jit(solution)/shard_map/all_gather | solution.py:83
  352.5 181.9 %copy-start.2 = (f32[4,512,128,16]{2,1,3,0:T(8,128)}, f32[4,512,128,16]{2,1,3,0:T(8,128)S(1)}, u32[]{:S(2)}) copy-start(f32[4,512,128,16]{2,1,3,0:T(8,128)S(1)} %get-tuple-element.111) | copy-start | bytes 50331652
  352.5 15.9 %copy-start.7 = (bf16[512,4,128]{2,1,0:T(4,128)(2,1)S(1)}, bf16[512,4,128]{2,1,0:T(4,128)(2,1)}, u32[]{:S(2)}) copy-start(bf16[512,4,128]{2,1,0:T(4,128)(2,1)} %reshape.1145) | copy-start | bytes 1572868
  360.7 15.4 %copy-start.6 = (bf16[512,4,128]{2,1,0:T(4,128)(2,1)S(1)}, bf16[512,4,128]{2,1,0:T(4,128)(2,1)}, u32[]{:S(2)}) copy-start(bf16[512,4,128]{2,1,0:T(4,128)(2,1)} %reshape.1143) | copy-start | bytes 1572868
  368.4 15.3 %copy-start.5 = (bf16[512,4,128]{2,1,0:T(4,128)(2,1)S(1)}, bf16[512,4,128]{2,1,0:T(4,128)(2,1)}, u32[]{:S(2)}) copy-start(bf16[512,4,128]{2,1,0:T(4,128)(2,1)} %reshape.1141) | copy-start | bytes 1572868
  368.4 15.3 %copy-start.10 = (pred[128,512]{0,1:T(8,128)(4,1)S(1)}, pred[128,512]{0,1:T(8,128)(4,1)}, u32[]{:S(2)}) copy-start(pred[128,512]{0,1:T(8,128)(4,1)} %get-tuple-element.70) | copy-start | bytes 196612
  376.2 15.2 %copy-start.11 = (pred[128,512]{0,1:T(8,128)(4,1)S(1)}, pred[128,512]{0,1:T(8,128)(4,1)}, u32[]{:S(2)}) copy-start(pred[128,512]{0,1:T(8,128)(4,1)} %get-tuple-element.72) | copy-start | bytes 196612
  383.7 15.1 %copy-start.4 = (bf16[512,4,128]{2,1,0:T(4,128)(2,1)S(1)}, bf16[512,4,128]{2,1,0:T(4,128)(2,1)}, u32[]{:S(2)}) copy-start(bf16[512,4,128]{2,1,0:T(4,128)(2,1)} %reshape.1151) | copy-start | bytes 1572868
  391.3 15.2 %copy-start.19 = (f32[128,512]{0,1:T(8,128)S(1)}, f32[128,512]{0,1:T(8,128)}, u32[]{:S(2)}) copy-start(f32[128,512]{0,1:T(8,128)} %get-tuple-element.73) | copy-start | bytes 786436
  391.3 15.2 %copy-start.27 = (bf16[512,512]{0,1:T(8,128)(2,1)S(1)}, bf16[512,512]{0,1:T(8,128)(2,1)}, u32[]{:S(2)}) copy-start(bf16[512,512]{0,1:T(8,128)(2,1)} %copy.137) | copy-start | bytes 1572868
  457.3 14.2 %copy-start.24 = (bf16[512,512]{0,1:T(8,128)(2,1)S(1)}, bf16[512,512]{0,1:T(8,128)(2,1)}, u32[]{:S(2)}) copy-start(bf16[512,512]{0,1:T(8,128)(2,1)} %copy.149) | copy-start | bytes 1572868
  570.8 170.6 %copy-start.1 = (bf16[5120,256]{1,0:T(8,128)(2,1)S(1)}, bf16[5120,256]{1,0:T(8,128)(2,1)}, u32[]{:S(2)}) copy-start(bf16[5120,256]{1,0:T(8,128)(2,1)} %param.14) | copy-start | bytes 7864324
  576.4 50.0 %collective-permute-start = (bf16[128,8192]{1,0:T(8,128)(2,1)}, bf16[128,8192]{1,0:T(8,128)(2,1)}, u32[]{:S(2)}, u32[]{:S(2)}) collective-permute-start(bf16[128,8192]{1,0:T(8,128)(2,1)} %broadcast_select_fusion), channel_id=1, source_target_pairs={{0,32},{32,64},{64,96},{1,33},{33,65},{65,97},{2,34},{34,66},{66,9... | collective-permute-start | bytes 6291464 | tf_op jit(solution)/shard_map/ppermute | solution.py:14
  632.0 49.2 %collective-permute-start.1 = (bf16[128,8192]{1,0:T(8,128)(2,1)}, bf16[128,8192]{1,0:T(8,128)(2,1)}, u32[]{:S(2)}, u32[]{:S(2)}) collective-permute-start(bf16[128,8192]{1,0:T(8,128)(2,1)} %broadcast_select_fusion.1), channel_id=1, source_target_pairs={{0,32},{32,64},{64,96},{1,33},{33,65},{65,97},{2,34},{34,66},{66,9... | collective-permute-start | bytes 6291464 | tf_op jit(solution)/shard_map/ppermute | solution.py:14
  686.7 48.2 %collective-permute-start.2 = (bf16[128,8192]{1,0:T(8,128)(2,1)}, bf16[128,8192]{1,0:T(8,128)(2,1)}, u32[]{:S(2)}, u32[]{:S(2)}) collective-permute-start(bf16[128,8192]{1,0:T(8,128)(2,1)} %broadcast_select_fusion.2), channel_id=1, source_target_pairs={{0,32},{32,64},{64,96},{1,33},{33,65},{65,97},{2,34},{34,66},{66,9... | collective-permute-start | bytes 6291464 | tf_op jit(solution)/shard_map/ppermute | solution.py:14
  (15 other events, 179.8 us)
Sparse Core Ops, SparseCore 0:
  9.6 45.6 all-gather.8
  61.1 48.5 all-gather.10
  112.0 52.3 all-gather.16
  166.5 52.3 all-gather.18
  221.0 45.5 all-gather.12
  268.7 45.3 all-gather.14
where the time goes:
time: 756 us; the launch traced here: 748 us
  waiting for transfers between devices  393 us (52%)
  matrix products  182 us (24%)
  other arithmetic  103 us (14%)
  local copies, waits for them, and re-layouts  52.3 us (7%)
  between operations  14.1 us (2%)
    ppermute x3, waiting for transfers between devices, passed_along(): return lax.ppermute(block, axis, route)  144 us
    dot_general x8, matrix products, shards(): jnp.einsum('tkgn,nkd->tkgd', expo, value_block.astype(jnp.float32))  106 us
    dot_general x8, matrix products, shards(): jnp.einsum('tkgd,nkd->tkgn', query, key_block, preferred_element_type=jnp...  58.9 us
    reduce_sum x4, other arithmetic, shards(): total = total * shrink + jnp.sum(expo, axis=-1)  52.9 us
    all_gather x1, waiting for transfers between devices, shards(): lax.all_gather(w_key[0], 'ctx', axis=0, tiled=True)  50.6 us
    all_gather x1, waiting for transfers between devices, shards(): lax.all_gather(w_value[0], 'ctx', axis=0, tiled=True)  49.1 us
    all_gather x1, waiting for transfers between devices, shards(): lax.all_gather(patches, 'ctx', axis=0, tiled=True)  48 us
    all_gather x1, waiting for transfers between devices, shards(): lax.all_gather(values, 'ctx', axis=0, tiled=True)  42.4 us
  transfers between devices with their start and end apart: 9, of which 9 were waited for; matrix products, arithmetic and copies ran while one was open for 7% of the time, Pallas kernels for 0%

commit v1 on v0

v1 whole, which is shorter than its diff:
```python
import math

import jax
import jax.numpy as jnp
from jax import lax
from jax.experimental import pallas as pl
from jax.experimental.pallas import tpu as pltpu
from jax.sharding import PartitionSpec as P

QH = 64
HD = 128
MESH = pl.DeviceIdType.MESH
BIG = 1e30
CHUNK_HEADS = 4
WINDOW = 9


def attend_chain_kernel(
    q_ref, kt_ref, v_ref, kx_ref, qx_ref, joined_ref, out_ref,
    mixed, hidden, stage, landed, send_sem, recv_sem,
):
    section = lax.axis_index("section")
    sections = lax.axis_size("section")
    ctx = lax.axis_index("ctx")
    chip = ctx // 2
    core = ctx % 2
    chips = kt_ref.shape[0]
    tok = q_ref.shape[0]
    span = kt_ref.shape[2]
    width = CHUNK_HEADS * HD
    chunks = q_ref.shape[1] // width
    per_kv = 16 // CHUNK_HEADS
    rate = math.log2(math.e) / math.sqrt(HD)

    before = lax.rem(section + sections - 1, sections)
    after = lax.rem(section + 1, sections)
    barrier = pltpu.get_barrier_semaphore()
    pl.semaphore_signal(barrier, inc=1, device_id={"section": before}, device_id_type=MESH)
    pl.semaphore_wait(barrier, 1)

    def hop(c):
        return pltpu.make_async_remote_copy(
            src_ref=stage.at[c], dst_ref=landed.at[c],
            send_sem=send_sem.at[c], recv_sem=recv_sem.at[c],
            device_id={"section": after}, device_id_type=MESH,
        )

    def chain(c):
        cols = pl.ds(pl.multiple_of(c * width, width), width)

        @pl.when(section == 0)
        def _():
            hidden[...] = joined_ref[:, cols]

        @pl.when(section > 0)
        def _():
            hop(c).wait_recv()
            hidden[...] = landed[c]

        fresh = (hidden[...].astype(jnp.float32) + mixed[c]).astype(jnp.bfloat16)
        out_ref[:, cols] = fresh

        @pl.when(section < sections - 1)
        def _():
            stage[c] = fresh
            hop(c).start()

    def attend(i):
        kv = i // per_kv
        kcols = pl.ds(pl.multiple_of(kv * HD, HD), HD)
        where = [lax.rem(chip + (chips - WINDOW + 1) + w, chips) for w in range(WINDOW)]
        kc = [jnp.concatenate([kt_ref[b, kcols, :], kx_ref[b]], axis=0) for b in where]
        ones = jnp.ones((span, HD), jnp.bfloat16)
        vc = [jnp.concatenate([v_ref[b, :, kcols], ones], axis=1) for b in where]
        kc = jnp.concatenate(kc, axis=1)
        vc = jnp.concatenate(vc, axis=0)
        last = (WINDOW - 1) * span
        row = lax.broadcasted_iota(jnp.int32, (tok, span), 0) + core * tok
        col = lax.broadcasted_iota(jnp.int32, (tok, span), 1)
        for h in range(CHUNK_HEADS):
            qh = q_ref[:, pl.ds(pl.multiple_of(i * width, width) + h * HD, HD)]
            qc = jnp.concatenate([qh, qx_ref[...]], axis=1)
            s = jnp.dot(qc, kc, preferred_element_type=jnp.float32)
            own = jnp.where(col <= row, s[:, last:], -BIG)
            s = jnp.concatenate([s[:, :last], own], axis=1)
            top = jnp.max(s, axis=1, keepdims=True)
            p = jnp.exp2((s - top) * rate).astype(jnp.bfloat16)
            r = jnp.dot(p, vc, preferred_element_type=jnp.float32)
            mixed[i, :, h * HD : (h + 1) * HD] = r[:, :HD] / r[:, HD:]

    def step(i, _):
        attend(i)
        c = i - section

        @pl.when(c >= 0)
        def _():
            chain(c)

        return 0

    lax.fori_loop(0, chunks, step, 0)

    def tail(i, _):
        c = i - section

        @pl.when(c < chunks)
        def _():
            chain(c)

        return 0

    lax.fori_loop(chunks, chunks + sections - 1, tail, 0)

    @pl.when(section < sections - 1)
    def _():
        def drain(c, _):
            hop(c).wait_send()
            return 0

        lax.fori_loop(0, chunks, drain, 0)


def attend_chain(query, keys_t, values, key_marks, query_marks, joined):
    tok, width = query.shape
    cols = CHUNK_HEADS * HD
    chunks = width // cols
    vmem = pl.BlockSpec(memory_space=pltpu.VMEM)
    return pl.pallas_call(
        attend_chain_kernel,
        out_shape=jax.ShapeDtypeStruct((tok, width), jnp.bfloat16),
        in_specs=[vmem] * 6,
        out_specs=vmem,
        scratch_shapes=[
            pltpu.VMEM((chunks, tok, cols), jnp.float32),
            pltpu.VMEM((tok, cols), jnp.bfloat16),
            pltpu.VMEM((chunks, tok, cols), jnp.bfloat16),
            pltpu.VMEM((chunks, tok, cols), jnp.bfloat16),
            pltpu.SemaphoreType.DMA((chunks,)),
            pltpu.SemaphoreType.DMA((chunks,)),
        ],
        compiler_params=pltpu.CompilerParams(
            collective_id=1, has_side_effects=True, vmem_limit_bytes=56 * 2**20
        ),
        cost_estimate=pl.CostEstimate(
            flops=4 * tok * width * 2304, bytes_accessed=20 * 2**20, transcendentals=tok * 64 * 2304
        ),
    )(query, keys_t, values, key_marks, query_marks, joined)


def marks(doc_ids, qdoc, chip, chips):
    lane = jnp.arange(HD, dtype=jnp.int32)
    kdoc = doc_ids.reshape(chips, 1, -1)
    later = (jnp.arange(chips, dtype=jnp.int32) > chip)[:, None, None]
    other = (kdoc != lane[None, :, None]) & (lane < 8)[None, :, None]
    key_marks = (other | (later & (lane == 8)[None, :, None])).astype(jnp.bfloat16)
    hit = (qdoc[:, None] == lane[None, :]) | (lane == 8)[None, :]
    query_marks = jnp.where(hit, -BIG, 0.0).astype(jnp.bfloat16)
    return key_marks, query_marks


def rms_norm(values, gain):
    wide = values.astype(jnp.float32)
    scale = lax.rsqrt(jnp.mean(wide * wide, axis=-1, keepdims=True) + 1e-06)
    return (wide * scale * gain).astype(jnp.bfloat16)


def shards(
    text_embeds,
    patches,
    vis_gain,
    w_merge,
    frame_count,
    frame_offset,
    doc_ids,
    norm_gain,
    w_key,
    w_value,
    queries,
):
    ctx_count = lax.axis_size("ctx")
    ctx_index = lax.axis_index("ctx")
    tok_count = text_embeds.shape[0]
    width = text_embeds.shape[1]
    slots = frame_offset.shape[0]
    slot_dev = slots // ctx_count
    column_part = jnp.dot(
        rms_norm(lax.all_gather(patches, "ctx", axis=0, tiled=True), vis_gain),
        w_merge,
        preferred_element_type=jnp.float32,
    ).astype(jnp.bfloat16)
    vision_rows = column_part.shape[0]
    frame_tok = vision_rows // slots
    row_index = jnp.arange(vision_rows, dtype=jnp.int32)
    slot = row_index // frame_tok
    owner = slot // slot_dev
    used = slot % slot_dev < frame_count[owner]
    dest = frame_offset[slot] + row_index % frame_tok
    own_pos = ctx_index * tok_count + jnp.arange(tok_count, dtype=jnp.int32)
    own_match = (dest[None, :] == own_pos[:, None]) & used[None, :]
    covered = jnp.any(own_match, axis=1)
    full_rows = lax.all_gather(column_part, "ctx", axis=1, tiled=True)
    placed = jnp.dot(
        own_match.astype(jnp.bfloat16), full_rows, preferred_element_type=jnp.float32
    ).astype(jnp.bfloat16)
    joined = jnp.where(covered[:, None], placed, text_embeds)
    kv_width = w_key.shape[2]
    qdoc = lax.dynamic_slice_in_dim(doc_ids, ctx_index * tok_count, tok_count, 0)
    normed = rms_norm(joined, norm_gain[0])
    pieces = (
        lax.all_gather(w_key[0], "ctx", axis=0, tiled=True),
        lax.all_gather(w_value[0], "ctx", axis=0, tiled=True),
    )
    key_sum = jnp.dot(normed, pieces[0], preferred_element_type=jnp.float32)
    value_sum = jnp.dot(normed, pieces[1], preferred_element_type=jnp.float32)
    keys = key_sum.astype(jnp.bfloat16)
    values = value_sum.astype(jnp.bfloat16)
    all_keys, all_values = (
        lax.all_gather(keys, "ctx", axis=0, tiled=True),
        lax.all_gather(values, "ctx", axis=0, tiled=True),
    )
    chips = ctx_count // 2
    keys_t = all_keys.reshape(chips, 2 * tok_count, kv_width).transpose(0, 2, 1)
    values_b = all_values.reshape(chips, 2 * tok_count, kv_width)
    key_marks, query_marks = marks(doc_ids, qdoc, ctx_index // 2, chips)
    result = attend_chain(queries[0], keys_t, values_b, key_marks, query_marks, joined)
    return result.reshape(1, tok_count, width)


def solution(mesh):
    return jax.shard_map(
        shards,
        mesh=mesh,
        in_specs=(
            P("ctx", None),
            P("ctx", None),
            P(),
            P(None, "ctx"),
            P(),
            P(),
            P(),
            P("section", None),
            P("section", "ctx", None),
            P("section", "ctx", None),
            P("section", "ctx", None),
        ),
        out_specs=P("section", "ctx", None),
        check_vma=False,
    )
```

time: 756 us -> 390 us (0.52)
  matrix products: 182 us -> 20.5 us
  waiting for transfers between devices: 393 us -> 251 us
  other arithmetic: 103 us -> 25.8 us
  Pallas kernels: 0 us -> 64.9 us
  local copies, waits for them, and re-layouts: 52.3 us -> 12.9 us
    dot_general x16 -> x0, matrix products: 164 us -> none  [the longest x8 106 us: shards(): jnp.einsum('tkgn,nkd->tkgd', expo, value_block.astype(jnp.float32))]
    ppermute x3 -> x0, waiting for transfers between devices: 144 us -> none  [passed_along(): return lax.ppermute(block, axis, route)]
    pallas_call x0 -> x1, Pallas kernels: none -> 64.9 us  [attend_chain(): pl.pallas_call(attend_chain_kernel, out_shape=jax.ShapeDtypeStruct((tok,...]
    reduce_sum x4 -> x0, other arithmetic: 52.9 us -> none  [shards(): total = total * shrink + jnp.sum(expo, axis=-1)]
    reshape x17 -> x1, local copies, waits for them, and re-layouts: 36 us -> 6.39 us  [shards(): keys_t = all_keys.reshape(chips, 2 * tok_count, kv_width).transpose(0, 2, 1)]
    select_n x3 -> x0, other arithmetic: 16.7 us -> none  [shards(): carried = jnp.where(section_index == turn, updated, carried)]
    slice x2 -> x0, local copies, waits for them, and re-layouts: 8.1 us -> none  [the longest x1 4.13 us: shards(): pieces[1][block * step:(block + 1) * step]]
  transfers between devices with their start and end apart: 9 -> 6, of which waited for: 9 -> 6; matrix products, arithmetic and copies ran while one was open for 7% -> 13% of each run, Pallas kernels for 0% -> 0%
where the time goes in v1:
time: 390 us; the launch traced here: 389 us
  waiting for transfers between devices  251 us (64%)
  Pallas kernels  64.9 us (17%)
  other arithmetic  25.8 us (7%)
  matrix products  20.5 us (5%)
  between operations  13.6 us (3%)
  local copies, waits for them, and re-layouts  12.9 us (3%)
    pallas_call x1, Pallas kernels, attend_chain(): pl.pallas_call(attend_chain_kernel, out_shape=jax.ShapeDtypeStruct((tok,...  64.9 us
    all_gather x1, waiting for transfers between devices, shards(): lax.all_gather(w_key[0], 'ctx', axis=0, tiled=True)  49.4 us
    all_gather x1, waiting for transfers between devices, shards(): lax.all_gather(w_value[0], 'ctx', axis=0, tiled=True)  48.5 us
    all_gather x1, waiting for transfers between devices, shards(): lax.all_gather(patches, 'ctx', axis=0, tiled=True)  48 us
    all_gather x1, waiting for transfers between devices, shards(): lax.all_gather(values, 'ctx', axis=0, tiled=True)  41.1 us
    all_gather x1, waiting for transfers between devices, shards(): lax.all_gather(keys, 'ctx', axis=0, tiled=True)  39.5 us
    all_gather x1, waiting for transfers between devices, shards(): full_rows = lax.all_gather(column_part, 'ctx', axis=1, tiled=True)  22.6 us
    lt x1, other arithmetic, shards(): used = slot % slot_dev < frame_count[owner]  15.7 us
  transfers between devices with their start and end apart: 6, of which 6 were waited for; matrix products, arithmetic and copies ran while one was open for 13% of the time, Pallas kernels for 0%

profile of v1, /device:TPU:96, one launch (start us, length us, event | category | flops | bytes accessed | tf_op | source)
XLA Modules:
  0.0 388.9 jit_solution(7736648296003079119)
XLA Ops:
  6.5 0.7 all-gather.9.cloned.1.call-update
  7.3 48.0 %all-gather.9.cloned.1.call-done = bf16[256,5120]{1,0:T(8,128)(2,1)} async-done(((bf16[8,5120]{1,0:T(8,128)(2,1)}), bf16[256,5120]{1,0:T(8,128)(2,1)}) %all-gather.9.cloned.1.call-update) | async-done | bytes 2621456 | tf_op jit(solution)/shard_map/all_gather | solution.py:187
  55.3 2.3 fusion.5
  57.7 3.3 fusion.18
  61.0 0.7 all-gather.17.cloned.1.call-update
  61.8 0.5 all-gather.19.cloned.1.call-update
  62.4 1.9 gather_fusion
  65.3 0.7 fusion.39
  66.0 4.4 %compare_select_fusion.1 = s32[256,1]{0,1:T(1,128)S(1)} fusion(s32[]{:T(128)} %bitcast.27, s32[]{:T(128)} %bitcast.28, s32[]{:T(128)} %bitcast.29, s32[]{:T(128)} %bitcast.30, s32[]{:T(128)} %bitcast.31, s32[]{:T(128)} %bitcast.33, s32[]{:T(128)} %bitcast.32), kind=kLoop, calls=%fused_computation.62 | loop fusion | flops 9728 | bytes 1052 | tf_op jit(solution)/shard_map/gather | solution.py:196
  70.5 0.7 fusion.38
  71.2 15.7 %fusion.34 = pred[256]{0:T(512)(128)(4,1)S(1)} fusion(pred[256]{0:T(512)(128)(4,1)S(1)} %compare_reduce_fusion, pred[256]{0:T(512)(128)(4,1)S(1)} %compare_reduce_fusion.1, pred[256]{0:T(512)(128)(4,1)S(1)} %compare_reduce_fusion.2, pred[256]{0:T(512)(128)(4,1)S(1)} %compare_reduce_fusion.3, pred[256]{0:T(512)(128)(4,1)S(1)} %compare_reduce_fusion.4, ...), kind=kLoop, calls=%fused_computation.85 | loop fusion | flops 11520 | bytes 7780 | tf_op jit(solution)/shard_map/lt | solution.py:196
  87.1 22.6 %all-gather.11.cloned.1.call-done = bf16[256,8192]{1,0:T(8,128)(2,1)} async-done(((bf16[256,256]{1,0:T(8,128)(2,1)}), bf16[256,8192]{1,0:T(8,128)(2,1)}) %all-gather.11.cloned.1.call-update) | async-done | bytes 4194320 | tf_op jit(solution)/shard_map/all_gather | solution.py:201
  109.7 5.3 %fusion.8 = (f32[128]{0:T(128)S(1)}, bf16[128,8192]{1,0:T(8,128)(2,1)}) fusion(bf16[128,8192]{1,0:T(8,128)(2,1)} %param.11, bf16[256,8192]{1,0:T(8,128)(2,1)} %all-gather.11.cloned.1.call-done, s32[256]{0:T(256)S(1)} %fusion.35, s32[128]{0:T(128)S(1)} %iota_add_fusion, pred[256]{0:T(512)(128)(4,1)S(1)} %fusion.34, pred[128]{0:T(512)(128)(4,1)S(1)} %fusion.29), kind=kOutput, calls=%fused_computation.14 | convolution fusion | flops 542179200 | bytes 8391040 | tf_op jit(solution)/shard_map/dot_general | solution.py:202
  115.0 49.4 %all-gather.17.cloned.1.call-done = bf16[1,8192,512]{2,1,0:T(8,128)(2,1)} async-done(((bf16[1,256,512]{2,1,0:T(8,128)(2,1)}), bf16[1,8192,512]{2,1,0:T(8,128)(2,1)}) %all-gather.17.cloned.1.call-update) | async-done | bytes 8388624 | tf_op jit(solution)/shard_map/all_gather | solution.py:210
  164.3 6.0 %fusion.21 = bf16[128,512]{1,0:T(8,128)(2,1)} fusion(bf16[1,8192,512]{2,1,0:T(8,128)(2,1)} %all-gather.17.cloned.1.call-done, bf16[128,8192]{1,0:T(8,128)(2,1)} %get-tuple-element.38.joined_ref, f32[8192]{0:T(1024)S(1)} %bitcast.59, f32[128]{0:T(128)S(1)} %add_rsqrt_fusion.1), kind=kOutput, calls=%fused_computation.25 | convolution fusion | flops 1078001664 | bytes 10650112 | tf_op jit(solution)/shard_map/dot_general | solution.py:213
  170.4 48.5 %all-gather.19.cloned.1.call-done = bf16[1,8192,512]{2,1,0:T(8,128)(2,1)} async-done(((bf16[1,256,512]{2,1,0:T(8,128)(2,1)}), bf16[1,8192,512]{2,1,0:T(8,128)(2,1)}) %all-gather.19.cloned.1.call-update) | async-done | bytes 8388624 | tf_op jit(solution)/shard_map/all_gather | solution.py:211
  218.9 6.0 %fusion.24 = bf16[128,512]{1,0:T(8,128)(2,1)} fusion(bf16[1,8192,512]{2,1,0:T(8,128)(2,1)} %all-gather.19.cloned.1.call-done, bf16[128,8192]{1,0:T(8,128)(2,1)} %get-tuple-element.38.joined_ref, f32[8192]{0:T(1024)S(1)} %bitcast.60, f32[128]{0:T(128)S(1)} %add_rsqrt_fusion.1), kind=kOutput, calls=%fused_computation.26 | convolution fusion | flops 1078001664 | bytes 10650112 | tf_op jit(solution)/shard_map/dot_general | solution.py:214
  225.1 0.7 select_convert_fusion.qx_ref
  225.7 1.3 fusion.17.kx_ref
  227.1 39.5 %all-gather.13.cloned.1.call-done = bf16[4096,512]{1,0:T(8,128)(2,1)} async-done(((bf16[128,512]{1,0:T(8,128)(2,1)}), bf16[4096,512]{1,0:T(8,128)(2,1)}) %all-gather.13.cloned.1.call-update) | async-done | bytes 4194320 | tf_op jit(solution)/shard_map/all_gather | solution.py:218
  266.6 6.4 %copy.13 = bf16[16,256,512]{1,2,0:T(8,128)(2,1)} copy(bf16[16,256,512]{2,1,0:T(8,128)(2,1)} %bitcast.52) | data formatting | bytes 8388608 | tf_op jit(solution)/shard_map/reshape | solution.py:222
  273.0 41.1 %all-gather.15.cloned.1.call-done = bf16[4096,512]{1,0:T(8,128)(2,1)} async-done(((bf16[128,512]{1,0:T(8,128)(2,1)}), bf16[4096,512]{1,0:T(8,128)(2,1)}) %all-gather.15.cloned.1.call-update) | async-done | bytes 4194320 | tf_op jit(solution)/shard_map/all_gather | solution.py:219
  314.1 64.9 %shard_map.109 = bf16[128,8192]{1,0:T(8,128)(2,1)} custom-call(bf16[128,8192]{1,0:T(8,128)(2,1)} %bitcast.58, bf16[16,512,256]{2,1,0:T(8,128)(2,1)} %bitcast.53, bf16[16,256,512]{2,1,0:T(8,128)(2,1)} %bitcast.57, bf16[16,128,256]{2,1,0:T(8,128)(2,1)} %fusion.17.kx_ref, bf16[128,128]{1,0:T(8,128)(2,1)} %select_convert_fusion.qx_ref, ...), custom_call_target="tpu_custom_call" | custom-call | flops 9663676416 | bytes 20971520 | tf_op jit(solution)/shard_map/pallas_call | solution.py:128
  379.0 3.1 copy.15
  (57 shorter events, 1.7 us)
Async XLA Ops:
  6.5 51.1 %copy-start = (bf16[5120,256]{1,0:T(8,128)(2,1)S(1)}, bf16[5120,256]{1,0:T(8,128)(2,1)}, u32[]{:S(2)}) copy-start(bf16[5120,256]{1,0:T(8,128)(2,1)} %param.14) | copy-start | bytes 7864324
  6.5 48.8 %all-gather.9.cloned.1.call-start = ((), (), s32[]{:S(2)}) async-start(), calls=%async_computation | async-start | bytes 2703360 | tf_op jit(solution)/shard_map/all_gather | solution.py:187
  7.3 102.4 %all-gather.11.cloned.1.call-start = ((), (), s32[]{:S(2)}) async-start(), calls=%async_computation.1 | async-start | bytes 4325376 | tf_op jit(solution)/shard_map/all_gather | solution.py:201
  57.6 4.8 %copy-start.1 = (s32[64]{0:T(128)S(1)}, s32[64]{0:T(128)}, u32[]{:S(2)}) copy-start(s32[64]{0:T(128)} %param.16) | copy-start | bytes 772
  57.7 7.7 %copy-start.2 = (s32[32]{0:T(128)S(1)}, s32[32]{0:T(128)}, u32[]{:S(2)}) copy-start(s32[32]{0:T(128)} %param.15) | copy-start | bytes 388
  61.0 103.3 %all-gather.17.cloned.1.call-start = ((), (), s32[]{:S(2)}) async-start(), calls=%async_computation.4 | async-start | bytes 8650752 | tf_op jit(solution)/shard_map/all_gather | solution.py:210
  61.7 157.1 %all-gather.19.cloned.1.call-start = ((), (), s32[]{:S(2)}) async-start(), calls=%async_computation.5 | async-start | bytes 8650752 | tf_op jit(solution)/shard_map/all_gather | solution.py:211
  62.3 204.3 %all-gather.13.cloned.1.call-start = ((), (), s32[]{:S(2)}) async-start(), calls=%async_computation.2 | async-start | bytes 4325376 | tf_op jit(solution)/shard_map/all_gather | solution.py:218
  87.1 77.2 %copy-start.4 = (f32[1,8192]{1,0:T(1,128)S(1)}, f32[1,8192]{1,0:T(1,128)}, u32[]{:S(2)}) copy-start(f32[1,8192]{1,0:T(1,128)} %param.18) | copy-start | bytes 98308
  170.3 54.6 %copy-start.3 = (s32[4096]{0:T(1024)S(1)}, s32[4096]{0:T(1024)}, u32[]{:S(2)}) copy-start(s32[4096]{0:T(1024)} %param.17) | copy-start | bytes 49156
  170.3 143.8 %all-gather.15.cloned.1.call-start = ((), (), s32[]{:S(2)}) async-start(), calls=%async_computation.3 | async-start | bytes 4325376 | tf_op jit(solution)/shard_map/all_gather | solution.py:219
Sparse Core Ops, SparseCore 0:
  9.6 45.6 all-gather.8
  61.1 48.5 all-gather.10
  111.9 52.3 all-gather.16
  166.4 52.3 all-gather.18
  221.0 45.5 all-gather.12
  268.7 45.3 all-gather.14

commit v2 on v1

--- a/solution.py
+++ b/solution.py
@@ -16,7 +16,7 @@
 
 
 def attend_chain_kernel(
-    q_ref, kt_ref, v_ref, kx_ref, qx_ref, joined_ref, out_ref,
+    q_ref, kv_ref, kx_ref, qx_ref, joined_ref, out_ref,
     mixed, hidden, stage, landed, send_sem, recv_sem,
 ):
     section = lax.axis_index("section")
@@ -24,9 +24,9 @@
     ctx = lax.axis_index("ctx")
     chip = ctx // 2
     core = ctx % 2
-    chips = kt_ref.shape[0]
+    chips = kv_ref.shape[1]
     tok = q_ref.shape[0]
-    span = kt_ref.shape[2]
+    span = kv_ref.shape[3]
     width = CHUNK_HEADS * HD
     chunks = q_ref.shape[1] // width
     per_kv = 16 // CHUNK_HEADS
@@ -50,7 +50,7 @@
 
         @pl.when(section == 0)
         def _():
-            hidden[...] = joined_ref[:, cols]
+            hidden[...] = jnp.concatenate([joined_ref[2 * c], joined_ref[2 * c + 1]], axis=1)
 
         @pl.when(section > 0)
         def _():
@@ -68,10 +68,12 @@
     def attend(i):
         kv = i // per_kv
         kcols = pl.ds(pl.multiple_of(kv * HD, HD), HD)
+        vrows = pl.ds(pl.multiple_of(kv // 2 * span, span), span)
+        vcols = pl.ds(pl.multiple_of(lax.rem(kv, 2) * HD, HD), HD)
         where = [lax.rem(chip + (chips - WINDOW + 1) + w, chips) for w in range(WINDOW)]
-        kc = [jnp.concatenate([kt_ref[b, kcols, :], kx_ref[b]], axis=0) for b in where]
+        kc = [jnp.concatenate([kv_ref[0, b, kcols, :], kx_ref[b]], axis=0) for b in where]
         ones = jnp.ones((span, HD), jnp.bfloat16)
-        vc = [jnp.concatenate([v_ref[b, :, kcols], ones], axis=1) for b in where]
+        vc = [jnp.concatenate([kv_ref[1, b, vrows, vcols], ones], axis=1) for b in where]
         kc = jnp.concatenate(kc, axis=1)
         vc = jnp.concatenate(vc, axis=0)
         last = (WINDOW - 1) * span
@@ -120,7 +122,7 @@
         lax.fori_loop(0, chunks, drain, 0)
 
 
-def attend_chain(query, keys_t, values, key_marks, query_marks, joined):
+def attend_chain(query, keys_values, key_marks, query_marks, joined):
     tok, width = query.shape
     cols = CHUNK_HEADS * HD
     chunks = width // cols
@@ -128,7 +130,7 @@
     return pl.pallas_call(
         attend_chain_kernel,
         out_shape=jax.ShapeDtypeStruct((tok, width), jnp.bfloat16),
-        in_specs=[vmem] * 6,
+        in_specs=[vmem] * 5,
         out_specs=vmem,
         scratch_shapes=[
             pltpu.VMEM((chunks, tok, cols), jnp.float32),
@@ -144,7 +146,7 @@
         cost_estimate=pl.CostEstimate(
             flops=4 * tok * width * 2304, bytes_accessed=20 * 2**20, transcendentals=tok * 64 * 2304
         ),
-    )(query, keys_t, values, key_marks, query_marks, joined)
+    )(query, keys_values, key_marks, query_marks, joined)
 
 
 def marks(doc_ids, qdoc, chip, chips):
@@ -158,10 +160,461 @@
     return key_marks, query_marks
 
 
-def rms_norm(values, gain):
-    wide = values.astype(jnp.float32)
+def torus_gather(slot, own, place, part, send, recv):
+    y, x, core = place
+
+    def chip_at(r, q):
+        dy, dx = (q, r) if part == 0 else (r, q)
+        return lax.rem(y + dy + 4, 4) * 4 + lax.rem(x + dx + 4, 4)
+
+    table = {
+        "e0": (0, (0, 0), None, (1, 0), (-1, 0)),
+        "e1": (1, (0, 0), None, (-1, 0), (1, 0)),
+        "e2": (2, (-1, 0), 0, (1, 0), (2, 0)),
+        "e3": (3, (1, 0), 1, (-1, 0), (2, 0)),
+    }
+    for k, r in enumerate((0, -1, 1, 2)):
+        first = 4 + 4 * k
+        table["f0", r] = (first, (r, 0), None, (0, 1), (r, -1))
+        table["f1", r] = (first + 1, (r, 0), None, (0, -1), (r, 1))
+        table["f2", r] = (first + 2, (r, -1), 0, (0, 1), (r, 2))
+        table["f3", r] = (first + 3, (r, 1), 1, (0, -1), (r, 2))
+
+    def copy(event):
+        index, source, half, to, _ = table[event]
+        target = slot(chip_at(*source), half)
+        return pltpu.make_async_remote_copy(
+            src_ref=own(half) if source == (0, 0) else target,
+            dst_ref=target,
+            send_sem=send.at[part, index],
+            recv_sem=recv.at[part, index],
+            device_id={"ctx": chip_at(*to) * 2 + core},
+            device_id_type=MESH,
+        )
+
+    def start(*events):
+        for event in events:
+            copy(event).start()
+
+    def wait(*events):
+        for event in events:
+            index, _, half, _, landed = table[event]
+            target = slot(chip_at(*landed), half)
+            pltpu.make_async_copy(target, target, recv.at[part, index]).wait()
+
+    def drain():
+        for event in table:
+            copy(event).wait_send()
+
+    return start, wait, drain, chip_at
+
+
+def project_kernel(
+    patches_ref, vis_gain_ref, w_merge_ref, target_ref, pick_ref, text_ref, gain_ref,
+    w_key_ref, w_value_ref,
+    kv_ref, joined_out,
+    patch_buf, merged, rows_out, rows_in, text_buf, joined, normed, w_buf, acc, kv_own,
+    patch_send, patch_recv, w_send, w_recv, kv_send, kv_recv, pair_send, pair_recv,
+    row_sem, misc_send, misc_recv, local_sem,
+):
+    me = lax.axis_index("ctx")
+    count = lax.axis_size("ctx")
+    chip, core = me // 2, me % 2
+    y, x = chip // 4, chip % 4
+    place = (y, x, core)
+    sibling = chip * 2 + (1 - core)
+    tok = text_ref.shape[0]
+    chunk = joined.shape[2]
+
+    barrier = pltpu.get_barrier_semaphore()
+
+    def greet(i, _):
+        pl.semaphore_signal(
+            barrier, inc=1, device_id={"ctx": lax.rem(me + i, count)}, device_id_type=MESH
+        )
+        return 0
+
+    lax.fori_loop(1, count, greet, 0)
+
+    wide = patches_ref[...].astype(jnp.float32)
     scale = lax.rsqrt(jnp.mean(wide * wide, axis=-1, keepdims=True) + 1e-06)
-    return (wide * scale * gain).astype(jnp.bfloat16)
+    wide = wide * scale * vis_gain_ref[...]
+    half_in = wide.shape[1] // 2
+    patch_buf[core, chip] = jnp.concatenate(
+        [wide[:, :half_in], wide[:, half_in:]], axis=0
+    ).astype(jnp.bfloat16)
+
+    text_own = pltpu.make_async_copy(text_ref, text_buf.at[core], local_sem.at[0])
+    text_own.start()
+
+    def w_local(source):
+        return pltpu.make_async_copy(source, w_buf.at[me], local_sem.at[1])
+
+    @pl.when(core == 0)
+    def _():
+        w_local(w_key_ref).start()
+
+    @pl.when(core == 1)
+    def _():
+        w_local(w_value_ref).start()
+
+    pl.semaphore_wait(barrier, count - 1)
+
+    def patch_slot(part):
+        def at(c, half):
+            quarter = half_in // 4
+            if half is None:
+                cols = pl.ds(part * 2 * quarter, 2 * quarter)
+            else:
+                cols = pl.ds((part * 2 + half) * quarter, quarter)
+            return patch_buf.at[core, c, :, cols]
+
+        return at
+
+    def patch_own(part):
+        return lambda half: patch_slot(part)(chip, half)
+
+    def w_slot(part):
+        def at(c, half):
+            if half is None:
+                return w_buf.at[c * 2 + part]
+            return w_buf.at[c * 2 + part, pl.ds(half * 128, 128), :]
+
+        return at
+
+    def w_own(part):
+        return lambda half: w_slot(part)(chip, half)
+
+    both = range(2)
+    patch = [
+        torus_gather(patch_slot(p), patch_own(p), place, p, patch_send, patch_recv) for p in both
+    ]
+    w = [torus_gather(w_slot(p), w_own(p), place, p, w_send, w_recv) for p in both]
+
+    for start, *_ in patch:
+        start("e0", "e1", ("f0", 0), ("f1", 0))
+
+    def to_sibling(src, dst, k):
+        return pltpu.make_async_remote_copy(
+            src_ref=src, dst_ref=dst, send_sem=misc_send.at[k], recv_sem=misc_recv.at[k],
+            device_id={"ctx": sibling}, device_id_type=MESH,
+        )
+
+    @pl.when(core == 0)
+    def _():
+        to_sibling(w_value_ref, w_buf.at[me], 0).start()
+
+    @pl.when(core == 1)
+    def _():
+        to_sibling(w_key_ref, w_buf.at[me], 0).start()
+
+    text_pair = to_sibling(text_ref, text_buf.at[core], 1)
+    text_pair.start()
+
+    for start, wait, *_ in patch:
+        wait("e0")
+        start("e2", ("f0", -1), ("f1", -1))
+        wait("e1")
+        start("e3", ("f0", 1), ("f1", 1))
+
+    w_local(w_key_ref).wait()
+    pltpu.make_async_copy(w_buf.at[sibling], w_buf.at[sibling], misc_recv.at[0]).wait()
+    for start, *_ in w:
+        start("e0", "e1")
+
+    for start, wait, *_ in patch:
+        wait(("f0", 0))
+        start(("f2", 0))
+        wait(("f1", 0))
+        start(("f3", 0))
+    for start, wait, *_ in patch:
+        wait("e2", "e3")
+        start(("f0", 2), ("f1", 2))
+    for start, *_ in w:
+        start(("f0", 0), ("f1", 0))
+    for r in (-1, 1, 2):
+        for start, wait, *_ in patch:
+            wait(("f0", r))
+            start(("f2", r))
+            wait(("f1", r))
+            start(("f3", r))
+    for start, wait, *_ in patch:
+        for r in (0, -1, 1, 2):
+            wait(("f2", r), ("f3", r))
+    patch_pair = to_sibling(patch_buf.at[core], patch_buf.at[core], 2)
+    patch_pair.start()
+
+    for start, wait, *_ in w:
+        wait("e0")
+        start("e2", ("f0", -1), ("f1", -1))
+        wait("e1")
+        start("e3", ("f0", 1), ("f1", 1))
+
+    other = patch_buf.at[1 - core]
+    pltpu.make_async_copy(other, other, misc_recv.at[2]).wait()
+
+    group = 4
+    per = patch_buf.shape[1] // group
+
+    def merge(i, _):
+        rows = patch_buf[i // group, pl.ds(lax.rem(i, group) * per, per)]
+        flat = rows.reshape(per * 16, half_in)
+        low = jnp.dot(flat, w_merge_ref[:half_in, :], preferred_element_type=jnp.float32)
+        high = jnp.dot(flat, w_merge_ref[half_in:, :], preferred_element_type=jnp.float32)
+        width = low.shape[1]
+        low = low.reshape(per, 16, width)[:, :8]
+        high = high.reshape(per, 16, width)[:, 8:]
+        merged[pl.ds(pl.multiple_of(i * per * 8, per * 8), per * 8), :] = (
+            (low + high).reshape(per * 8, width).astype(jnp.bfloat16)
+        )
+        return 0
+
+    lax.fori_loop(0, 2 * group, merge, 0)
+
+    slots = rows_out.shape[1]
+    which = lax.broadcasted_iota(jnp.int32, (rows_out.shape[0] * slots, merged.shape[0]), 0)
+    choose = jnp.where(which == target_ref[...], 1.0, 0.0).astype(jnp.bfloat16)
+    chosen = jnp.dot(choose, merged[...], preferred_element_type=jnp.float32)
+    rows_out[...] = chosen.astype(jnp.bfloat16).reshape(rows_out.shape)
+    rows_in[me] = rows_out[chip]
+
+    def deliver(i, _):
+        to = lax.rem(me + i, count)
+        pltpu.make_async_remote_copy(
+            src_ref=rows_out.at[to // 2], dst_ref=rows_in.at[me],
+            send_sem=row_sem.at[0], recv_sem=row_sem.at[1],
+            device_id={"ctx": to}, device_id_type=MESH,
+        ).start()
+        return 0
+
+    lax.fori_loop(1, count, deliver, 0)
+
+    for start, wait, *_ in w:
+        wait(("f0", 0))
+        start(("f2", 0))
+        wait(("f1", 0))
+        start(("f3", 0))
+    for start, wait, *_ in w:
+        wait("e2", "e3")
+        start(("f0", 2), ("f1", 2))
+    for start, wait, *_ in w:
+        wait(("f0", -1))
+        start(("f2", -1))
+        wait(("f1", -1))
+        start(("f3", -1))
+
+    text_own.wait()
+    pltpu.make_async_copy(
+        text_buf.at[1 - core], text_buf.at[1 - core], misc_recv.at[1]
+    ).wait()
+    most = rows_in.at[pl.ds(0, count - 1)]
+    pltpu.make_async_copy(most, most, row_sem.at[0]).wait()
+    pltpu.make_async_copy(most, most, row_sem.at[1]).wait()
+
+    pick = pick_ref[...]
+    covered = jnp.sum(pick.astype(jnp.float32), axis=1, keepdims=True) > 0.0
+
+    def join(i, squares):
+        placed = jnp.dot(pick, rows_in[i], preferred_element_type=jnp.float32)
+        cols = pl.ds(pl.multiple_of(i * chunk, chunk), chunk)
+        text = text_buf[:, :, cols].reshape(2 * tok, chunk).astype(jnp.float32)
+        value = jnp.where(covered, placed, text)
+        joined[i] = value.astype(jnp.bfloat16)
+        return squares + value * value
+
+    squares = lax.fori_loop(
+        0, count, join, jnp.zeros((2 * tok, chunk), jnp.float32), unroll=2
+    )
+    mean = jnp.sum(squares, axis=1, keepdims=True) / (count * chunk)
+    factor = lax.rsqrt(mean + 1e-06)
+
+    def norm(i, _):
+        cols = pl.ds(pl.multiple_of(i * chunk, chunk), chunk)
+        value = joined[i].astype(jnp.float32)
+        normed[i] = (value * factor * gain_ref[:, cols]).astype(jnp.bfloat16)
+        joined_out[i] = joined[i, pl.ds(pl.multiple_of(core * tok, tok), tok), :]
+        return 0
+
+    lax.fori_loop(0, count, norm, 0, unroll=2)
+
+    for r in (1, 2):
+        for start, wait, *_ in w:
+            wait(("f0", r))
+            start(("f2", r))
+            wait(("f1", r))
+            start(("f3", r))
+
+    acc[...] = jnp.zeros_like(acc)
+
+    def project(k, _):
+        far = k // 4
+        far = lax.rem(jnp.where(far < 2, far, 5 - far), 4)
+        near = lax.rem(k, 4)
+        one = 2 * (lax.rem(y + far, 4) * 4 + near)
+        two = 2 * (near * 4 + lax.rem(x + far, 4)) + 1
+        left = jnp.concatenate([normed[one], normed[two]], axis=1)
+        right = jnp.concatenate([w_buf[one], w_buf[two]], axis=0)
+        acc[...] += jnp.dot(left, right, preferred_element_type=jnp.float32)
+        return 0
+
+    lax.fori_loop(0, 12, project, 0)
+    for r in (0, -1, 1, 2):
+        for start, wait, *_ in w:
+            wait(("f2", r), ("f3", r))
+    lax.fori_loop(12, 16, project, 0)
+
+    @pl.when(core == 0)
+    def _():
+        kv_own[...] = acc[...].T.astype(jnp.bfloat16)
+
+    @pl.when(core == 1)
+    def _():
+        width = acc.shape[1] // 2
+        kv_own[...] = jnp.concatenate([acc[:, :width], acc[:, width:]], axis=0).astype(
+            jnp.bfloat16
+        )
+
+    def kv_rows(part, half):
+        if half is None:
+            return pl.ds(part * 256, 256)
+        return pl.ds(part * 256 + half * 128, 128)
+
+    def kv_slot(part):
+        return lambda c, half: kv_ref.at[core, c, kv_rows(part, half), :]
+
+    def kv_mine(part):
+        return lambda half: kv_own.at[kv_rows(part, half), :]
+
+    kv = [torus_gather(kv_slot(p), kv_mine(p), place, p, kv_send, kv_recv) for p in both]
+    rings = {0: 0, -1: 1, 1: 2, 2: 3}
+
+    def cross(part, r, q):
+        chip_at = kv[part][3]
+        index = rings[r] * 4 + rings[q]
+        target = kv_slot(part)(chip_at(r, q), None)
+        return pltpu.make_async_remote_copy(
+            src_ref=kv_mine(part)(None) if (r, q) == (0, 0) else target,
+            dst_ref=target,
+            send_sem=pair_send.at[part, index],
+            recv_sem=pair_recv.at[part, index],
+            device_id={"ctx": sibling}, device_id_type=MESH,
+        )
+
+    own_copy = pltpu.make_async_copy(kv_own, kv_ref.at[core, chip], local_sem.at[2])
+    own_copy.start()
+    for start, *_ in kv:
+        start("e0", "e1", ("f0", 0), ("f1", 0))
+    for p in both:
+        cross(p, 0, 0).start()
+    for p in both:
+        start, wait, *_ = kv[p]
+        wait("e0")
+        start("e2", ("f0", -1), ("f1", -1))
+        cross(p, -1, 0).start()
+        wait("e1")
+        start("e3", ("f0", 1), ("f1", 1))
+        cross(p, 1, 0).start()
+
+    def second(p, r):
+        start, wait, *_ = kv[p]
+        wait(("f0", r))
+        start(("f2", r))
+        cross(p, r, -1).start()
+        wait(("f1", r))
+        start(("f3", r))
+        cross(p, r, 1).start()
+
+    for p in both:
+        second(p, 0)
+    for p in both:
+        start, wait, *_ = kv[p]
+        wait("e2", "e3")
+        start(("f0", 2), ("f1", 2))
+        cross(p, 2, 0).start()
+    for r in (-1, 1, 2):
+        for p in both:
+            second(p, r)
+    for r in (0, -1, 1, 2):
+        for p in both:
+            kv[p][1](("f2", r), ("f3", r))
+            cross(p, r, 2).start()
+
+    for part in both:
+        for r in rings:
+            for q in rings:
+                landed = kv_ref.at[1 - core, kv[part][3](r, q), kv_rows(part, None), :]
+                index = rings[r] * 4 + rings[q]
+                pltpu.make_async_copy(landed, landed, pair_recv.at[part, index]).wait()
+                cross(part, r, q).wait_send()
+    own_copy.wait()
+    for gather in (patch, w, kv):
+        for _, _, drain, _ in gather:
+            drain()
+    to_sibling(w_value_ref, w_buf.at[me], 0).wait_send()
+    text_pair.wait_send()
+    patch_pair.wait_send()
+
+
+def project(patches, vis_gain, w_merge, target, pick, text, gain, w_key, w_value):
+    count = lax.axis_size("ctx")
+    tok, width = text.shape
+    chunk = width // count
+    kv_width = w_key.shape[1]
+    chips = count // 2
+    vmem = pl.BlockSpec(memory_space=pltpu.VMEM)
+    hbm = pl.BlockSpec(memory_space=pl.ANY)
+    dma = pltpu.SemaphoreType.DMA
+    return pl.pallas_call(
+        project_kernel,
+        out_shape=(
+            jax.ShapeDtypeStruct((2, chips, kv_width, 2 * tok), jnp.bfloat16),
+            jax.ShapeDtypeStruct((count, tok, chunk), jnp.bfloat16),
+        ),
+        in_specs=[vmem] * 5 + [hbm, vmem] + [hbm] * 2,
+        out_specs=(hbm, vmem),
+        scratch_shapes=[
+            pltpu.VMEM((2, chips, 16, patches.shape[1] // 2), jnp.bfloat16),
+            pltpu.VMEM((count * 8, chunk), jnp.bfloat16),
+            pltpu.VMEM((chips, 32, chunk), jnp.bfloat16),
+            pltpu.VMEM((count, 32, chunk), jnp.bfloat16),
+            pltpu.VMEM((2, tok, width), jnp.bfloat16),
+            pltpu.VMEM((count, 2 * tok, chunk), jnp.bfloat16),
+            pltpu.VMEM((count, 2 * tok, chunk), jnp.bfloat16),
+            pltpu.VMEM((count, chunk, kv_width), jnp.bfloat16),
+            pltpu.VMEM((2 * tok, kv_width), jnp.float32),
+            pltpu.VMEM((kv_width, 2 * tok), jnp.bfloat16),
+        ]
+        + [dma((2, 20))] * 6
+        + [dma((2, 16))] * 2
+        + [dma((2,)), dma((3,)), dma((3,)), dma((3,))],
+        compiler_params=pltpu.CompilerParams(
+            collective_id=2, has_side_effects=True, vmem_limit_bytes=56 * 2**20
+        ),
+        cost_estimate=pl.CostEstimate(
+            flops=4 * 10**9, bytes_accessed=20 * 2**20, transcendentals=0
+        ),
+    )(patches, vis_gain, w_merge, target, pick, text, gain, w_key, w_value)
+
+
+def frame_places(frame_count, frame_offset, chip, tok):
+    owners = frame_count.shape[0]
+    per = frame_offset.shape[0] // owners
+    used = (jnp.arange(per)[None, :] < frame_count[:, None]).reshape(-1)
+    block = frame_offset // tok
+    slot = jnp.arange(frame_offset.shape[0])
+    same = (block[None, :] == block[:, None]) & (slot[None, :] < slot[:, None])
+    rank = jnp.sum(same, axis=1, dtype=jnp.int32)
+    frame_tok = 4
+    row = jnp.arange(frame_tok, dtype=jnp.int32)
+    target = jnp.where(used, block * 16 + rank * frame_tok, -1000)[:, None] + row
+    dest = frame_offset[:, None] + row
+    target, dest = target.reshape(-1), dest.reshape(-1)
+    lane = jnp.arange(32, dtype=jnp.int32) + chip * 32
+    pos = jnp.arange(2 * tok, dtype=jnp.int32) + chip * 2 * tok
+    hit = (target[None, :] == lane[:, None])[None] & (dest[None, :] == pos[:, None])[:, None]
+    pick = jnp.any(hit, axis=2).astype(jnp.bfloat16)
+    order = target.reshape(owners // 2, 2, -1).transpose(1, 0, 2).reshape(1, -1)
+    return order, pick
 
 
 def shards(
@@ -177,53 +630,17 @@
     w_value,
     queries,
 ):
-    ctx_count = lax.axis_size("ctx")
     ctx_index = lax.axis_index("ctx")
-    tok_count = text_embeds.shape[0]
-    width = text_embeds.shape[1]
-    slots = frame_offset.shape[0]
-    slot_dev = slots // ctx_count
-    column_part = jnp.dot(
-        rms_norm(lax.all_gather(patches, "ctx", axis=0, tiled=True), vis_gain),
-        w_merge,
-        preferred_element_type=jnp.float32,
-    ).astype(jnp.bfloat16)
-    vision_rows = column_part.shape[0]
-    frame_tok = vision_rows // slots
-    row_index = jnp.arange(vision_rows, dtype=jnp.int32)
-    slot = row_index // frame_tok
-    owner = slot // slot_dev
-    used = slot % slot_dev < frame_count[owner]
-    dest = frame_offset[slot] + row_index % frame_tok
-    own_pos = ctx_index * tok_count + jnp.arange(tok_count, dtype=jnp.int32)
-    own_match = (dest[None, :] == own_pos[:, None]) & used[None, :]
-    covered = jnp.any(own_match, axis=1)
-    full_rows = lax.all_gather(column_part, "ctx", axis=1, tiled=True)
-    placed = jnp.dot(
-        own_match.astype(jnp.bfloat16), full_rows, preferred_element_type=jnp.float32
-    ).astype(jnp.bfloat16)
-    joined = jnp.where(covered[:, None], placed, text_embeds)
-    kv_width = w_key.shape[2]
-    qdoc = lax.dynamic_slice_in_dim(doc_ids, ctx_index * tok_count, tok_count, 0)
-    normed = rms_norm(joined, norm_gain[0])
-    pieces = (
-        lax.all_gather(w_key[0], "ctx", axis=0, tiled=True),
-        lax.all_gather(w_value[0], "ctx", axis=0, tiled=True),
+    tok, width = text_embeds.shape
+    chip = ctx_index // 2
+    order, pick = frame_places(frame_count, frame_offset, chip, tok)
+    qdoc = lax.dynamic_slice_in_dim(doc_ids, ctx_index * tok, tok, 0)
+    key_marks, query_marks = marks(doc_ids, qdoc, chip, lax.axis_size("ctx") // 2)
+    kv, joined = project(
+        patches, vis_gain[None], w_merge, order, pick, text_embeds, norm_gain, w_key[0], w_value[0]
     )
-    key_sum = jnp.dot(normed, pieces[0], preferred_element_type=jnp.float32)
-    value_sum = jnp.dot(normed, pieces[1], preferred_element_type=jnp.float32)
-    keys = key_sum.astype(jnp.bfloat16)
-    values = value_sum.astype(jnp.bfloat16)
-    all_keys, all_values = (
-        lax.all_gather(keys, "ctx", axis=0, tiled=True),
-        lax.all_gather(values, "ctx", axis=0, tiled=True),
-    )
-    chips = ctx_count // 2
-    keys_t = all_keys.reshape(chips, 2 * tok_count, kv_width).transpose(0, 2, 1)
-    values_b = all_values.reshape(chips, 2 * tok_count, kv_width)
-    key_marks, query_marks = marks(doc_ids, qdoc, ctx_index // 2, chips)
-    result = attend_chain(queries[0], keys_t, values_b, key_marks, query_marks, joined)
-    return result.reshape(1, tok_count, width)
+    result = attend_chain(queries[0], kv, key_marks, query_marks, joined)
+    return result[None]
 
 
 def solution(mesh):

time: 390 us -> 180 us (0.46)
  waiting for transfers between devices: 251 us -> 0 us
  Pallas kernels: 64.9 us -> 163 us
  matrix products: 20.5 us -> 0 us
  other arithmetic: 25.8 us -> 10.5 us
  between operations: 13.6 us -> 0.07 us
  local copies, waits for them, and re-layouts: 12.9 us -> 5.91 us
    all_gather x6 -> x0, waiting for transfers between devices: 249 us -> none  [the longest x1 49.4 us: shards(): lax.all_gather(w_key[0], 'ctx', axis=0, tiled=True)]
    pallas_call x0 -> x1, Pallas kernels: none -> 99.4 us  [project(): pl.pallas_call(project_kernel, out_shape=(jax.ShapeDtypeStruct((2, chips,...]
    dot_general x4 -> x0, matrix products: 20.5 us -> none  [the longest x1 5.98 us: shards(): value_sum = jnp.dot(normed, pieces[1], preferred_element_type=jnp.float32)]
    lt x1, other arithmetic: 15.7 us -> 0.73 us  [frame_places(): used = (jnp.arange(per)[None, :] < frame_count[:, None]).reshape(-1)]
    reshape x1, local copies, waits for them, and re-layouts: 6.39 us -> 0.64 us  [frame_places(): order = target.reshape(owners // 2, 2, -1).transpose(1, 0, 2).reshape(1, -1)]
    gather x27 -> x0, other arithmetic: 5.46 us -> none  [the longest x26 5.45 us: shards(): used = slot % slot_dev < frame_count[owner]]
    reduce_or x1, other arithmetic: 0.17 us -> 4.45 us  [frame_places(): pick = jnp.any(hit, axis=2).astype(jnp.bfloat16)]
  transfers between devices with their start and end apart: 6 -> 0, of which waited for: 6 -> 0; matrix products, arithmetic and copies ran while one was open for 13% -> 0% of each run, Pallas kernels for 0% -> 0%
where the time goes in v2:
time: 180 us
  Pallas kernels  163 us (91%)
  other arithmetic  10.5 us (6%)
  local copies, waits for them, and re-layouts  5.91 us (3%)
    pallas_call x1, Pallas kernels, project(): pl.pallas_call(project_kernel, out_shape=(jax.ShapeDtypeStruct((2, chips,...  99.4 us
    pallas_call x1, Pallas kernels, attend_chain(): pl.pallas_call(attend_chain_kernel, out_shape=jax.ShapeDtypeStruct((tok,...  63.8 us
    reduce_or x1, other arithmetic, frame_places(): pick = jnp.any(hit, axis=2).astype(jnp.bfloat16)  4.45 us

profile of v2, /device:TPU:96, one launch (start us, length us, event | category | flops | bytes accessed | tf_op | source)
XLA Modules:
  0.0 179.7 jit_solution(9109395757223355614)
XLA Ops:
  0.0 0.8 dynamic_slice.3
  0.8 0.7 and_select_fusion
  1.4 0.2 convert_reduce_fusion
  1.7 0.1 add.88
  1.8 0.7 iota_compare_fusion.3
  2.5 0.1 lt.43
  2.7 0.7 add_select_fusion
  3.3 0.1 add.84
  3.4 0.1 copy.15
  3.6 0.1 copy.16
  3.7 0.6 reshape.153.target_ref
  4.3 0.7 ne.42
  5.1 0.7 select_convert_fusion.qx_ref
  5.8 0.1 add.94
  5.9 0.1 broadcast_compare_fusion.1
  6.0 0.7 iota_add_fusion
  6.7 0.1 add.100
  6.8 0.1 broadcast_compare_fusion
  7.0 4.4 %and_reduce_fusion = pred[256,32]{1,0:T(8,128)(4,1)S(1)} fusion(pred[256,256]{1,0:T(8,128)(4,1)S(1)} %broadcast_compare_fusion, pred[32,256]{1,0:T(8,128)(4,1)S(1)} %broadcast_compare_fusion.1), kind=kLoop, calls=%fused_computation | loop fusion | flops 4186112 | bytes 81920 | tf_op jit(solution)/shard_map/reduce_or | solution.py:615
  11.4 0.6 convert_element_type.13.pick_ref
  12.1 1.3 fusion.2.kx_ref
  13.4 99.4 %shard_map.109 = (bf16[2,16,512,256]{3,2,1,0:T(8,128)(2,1)}, bf16[32,128,256]{2,1,0:T(8,128)(2,1)}) custom-call(bf16[8,5120]{1,0:T(8,128)(2,1)} %patches_ref.1, f32[1,5120]{1,0:T(1,128)} %bitcast.13, bf16[5120,256]{1,0:T(8,128)(2,1)} %w_merge_ref.1, s32[1,256]{1,0:T(1,128)} %reshape.153.target_ref, bf16[256,32]{1,0:T(8,128)(2,1)} %convert_element_type.13.pick_ref, ...), custom_call_target="tpu_custom_call" | custom-call | flops 4000000000 | bytes 20971520 | tf_op jit(solution)/shard_map/pallas_call | solution.py:567
  112.8 63.8 %shard_map.110 = bf16[128,8192]{1,0:T(8,128)(2,1)} custom-call(bf16[128,8192]{1,0:T(8,128)(2,1)} %bitcast.10, bf16[2,16,512,256]{3,2,1,0:T(8,128)(2,1)} %get-tuple-element.7.kv_ref, bf16[16,128,256]{2,1,0:T(8,128)(2,1)} %fusion.2.kx_ref, bf16[128,128]{1,0:T(8,128)(2,1)} %select_convert_fusion.qx_ref, bf16[32,128,256]{2,1,0:T(8,128)(2,1)} %get-tuple-element.8.joined_ref), custom_call_target="tpu_custom_call" | custom-call | flops 9663676416 | bytes 20971520 | tf_op jit(solution)/shard_map/pallas_call | solution.py:130
  176.6 3.1 %copy.18 = bf16[1,128,8192]{2,1,0:T(8,128)(2,1)} copy(bf16[1,128,8192]{2,1,0:T(8,128)(2,1)} %bitcast.8) | data formatting | bytes 4194304
  (10 shorter events, 0.3 us)

commit v3 on v1

v3 whole, which is shorter than its diff:
```python
import math

import jax
import jax.numpy as jnp
from jax import lax
from jax.experimental import pallas as pl
from jax.experimental.pallas import tpu as pltpu
from jax.sharding import PartitionSpec as P

QH = 64
HD = 128
MESH = pl.DeviceIdType.MESH
BIG = 1e30
CHUNK_HEADS = 4
WINDOW = 9
ROUNDS = 2


def torus_gather(slot, own, place, part, send, recv, round_=0):
    y, x, core = place

    def chip_at(r, q):
        dy, dx = (q, r) if part == 0 else (r, q)
        return lax.rem(y + dy + 4, 4) * 4 + lax.rem(x + dx + 4, 4)

    table = {
        "e0": (0, (0, 0), None, (1, 0), (-1, 0)),
        "e1": (1, (0, 0), None, (-1, 0), (1, 0)),
        "e2": (2, (-1, 0), 0, (1, 0), (2, 0)),
        "e3": (3, (1, 0), 1, (-1, 0), (2, 0)),
    }
    for k, r in enumerate((0, -1, 1, 2)):
        first = 4 + 4 * k
        table["f0", r] = (first, (r, 0), None, (0, 1), (r, -1))
        table["f1", r] = (first + 1, (r, 0), None, (0, -1), (r, 1))
        table["f2", r] = (first + 2, (r, -1), 0, (0, 1), (r, 2))
        table["f3", r] = (first + 3, (r, 1), 1, (0, -1), (r, 2))

    def copy(event):
        index, source, half, to, _ = table[event]
        target = slot(chip_at(*source), half)
        return pltpu.make_async_remote_copy(
            src_ref=own(half) if source == (0, 0) else target,
            dst_ref=target,
            send_sem=send.at[2 * round_ + part, index],
            recv_sem=recv.at[2 * round_ + part, index],
            device_id={"ctx": chip_at(*to) * 2 + core},
            device_id_type=MESH,
        )

    def start(*events):
        for event in events:
            copy(event).start()

    def wait(*events):
        for event in events:
            index, _, half, _, landed = table[event]
            target = slot(chip_at(*landed), half)
            pltpu.make_async_copy(target, target, recv.at[2 * round_ + part, index]).wait()

    def drain():
        for event in table:
            copy(event).wait_send()

    return start, wait, drain, chip_at


def one_hot(condition):
    return jnp.where(condition, 1.0, 0.0).astype(jnp.bfloat16)


def iota(shape, dim):
    return lax.broadcasted_iota(jnp.int32, shape, dim)


def frame_places(counts, offsets, chip):
    frames = offsets.shape[1]
    owners = counts.shape[1]
    rows = frames * 4
    block = offsets // 128
    within = (offsets - block * 128) // 4
    member = one_hot(iota((owners, frames), 0) == block)
    earlier = one_hot(iota((frames, frames), 0) < iota((frames, frames), 1))
    before = jnp.dot(member, earlier, preferred_element_type=jnp.float32)
    rank = jnp.sum(before * member.astype(jnp.float32), axis=0, keepdims=True)
    spread = one_hot(iota((owners, frames), 0) == iota((owners, frames), 1) // 2)
    count8 = jnp.broadcast_to(counts, (8, owners)).astype(jnp.float32).astype(jnp.bfloat16)
    count = jnp.dot(count8, spread, preferred_element_type=jnp.float32)
    used = jnp.where((iota((8, frames), 1) % 2).astype(jnp.float32) < count, 1.0, 0.0)
    line = iota((8, frames), 0)
    facts = jnp.where(
        line == 0,
        block.astype(jnp.float32),
        jnp.where(line == 1, rank, jnp.where(line == 2, within.astype(jnp.float32), used)),
    ).astype(jnp.bfloat16)
    place = iota((frames, rows), 1)
    row = place % 8
    frame = ((place % 128) // 8 * 2 + place // 128) * 2 + row // 4
    expand = one_hot(iota((frames, rows), 0) == frame)
    facts = jnp.dot(facts, expand, preferred_element_type=jnp.float32).astype(jnp.int32)
    low = iota((1, rows), 1) % 4
    target = jnp.where(facts[3:4] > 0, facts[0:1] * 16 + facts[1:2] * 4 + low, -1000)
    dest = facts[0:1] * 128 + facts[2:3] * 4 + low
    choose = one_hot(iota((owners * 16, rows), 0) == target)
    hot = one_hot(iota((32, rows), 0) + chip * 32 == target)
    spot = one_hot(iota((256, rows), 0) + chip * 256 == dest)
    pick = lax.dot_general(
        spot, hot, (((1,), (1,)), ((), ())), preferred_element_type=jnp.float32
    ).astype(jnp.bfloat16)
    return choose, pick


def window_kernel(
    patches_ref, vis_gain_ref, w_merge_hbm, count_ref, offset_ref, doc_ref, text_ref, gain_ref,
    w_key_ref, w_value_ref, query_hbm,
    out_ref,
    patch_buf, w_merge_ref, merged, rows_out, rows_in, text_buf, joined, normed, w_buf, acc, kv_own,
    kv_buf, q_ref, pick_ref, kx, qx, mixed, hidden, stage, landed,
    patch_send, patch_recv, w_send, w_recv, kv_send, kv_recv, pair_send, pair_recv,
    row_sem, misc_send, misc_recv, local_sem, hop_send, hop_recv,
):
    me = lax.axis_index("ctx")
    count = lax.axis_size("ctx")
    section = lax.axis_index("section")
    sections = lax.axis_size("section")
    chip, core = me // 2, me % 2
    y, x = chip // 4, chip % 4
    place = (y, x, core)
    sibling = chip * 2 + (1 - core)
    tok = text_ref.shape[0]
    chunk = joined.shape[2]
    chips = kv_buf.shape[1]
    span = kv_buf.shape[3]

    barrier = pltpu.get_barrier_semaphore()

    def greet(i, _):
        pl.semaphore_signal(
            barrier, inc=1, device_id={"ctx": lax.rem(me + i, count)}, device_id_type=MESH
        )
        return 0

    lax.fori_loop(1, count, greet, 0)
    before = lax.rem(section + sections - 1, sections)
    after = lax.rem(section + 1, sections)
    pl.semaphore_signal(barrier, inc=1, device_id={"section": before}, device_id_type=MESH)

    text_own = pltpu.make_async_copy(text_ref, text_buf.at[core], local_sem.at[0])
    w_merge_in = pltpu.make_async_copy(w_merge_hbm, w_merge_ref, local_sem.at[2])
    query_in = pltpu.make_async_copy(query_hbm, q_ref, local_sem.at[3])

    def w_local(source):
        return pltpu.make_async_copy(source, w_buf.at[me], local_sem.at[1])

    @pl.when(core == 0)
    def _():
        w_local(w_key_ref).start()

    @pl.when(core == 1)
    def _():
        w_local(w_value_ref).start()

    w_merge_in.start()
    text_own.start()
    query_in.start()

    wide = patches_ref[...].astype(jnp.float32)
    scale = lax.rsqrt(jnp.mean(wide * wide, axis=-1, keepdims=True) + 1e-06)
    wide = wide * scale * vis_gain_ref[...]
    half_in = wide.shape[1] // 2
    patch_buf[core, chip] = jnp.concatenate(
        [wide[:, :half_in], wide[:, half_in:]], axis=0
    ).astype(jnp.bfloat16)

    pl.semaphore_wait(barrier, count)

    def patch_slot(part):
        def at(c, half):
            quarter = half_in // 4
            if half is None:
                cols = pl.ds(part * 2 * quarter, 2 * quarter)
            else:
                cols = pl.ds((part * 2 + half) * quarter, quarter)
            return patch_buf.at[core, c, :, cols]

        return at

    def own_of(slot):
        return lambda half: slot(chip, half)

    w_cols = w_buf.shape[2] // ROUNDS

    def w_slot(part, turn):
        cols = pl.ds(turn * w_cols, w_cols)

        def at(c, half):
            rows = pl.ds(0, chunk) if half is None else pl.ds(half * (chunk // 2), chunk // 2)
            return w_buf.at[c * 2 + part, rows, cols]

        return at

    kv_part = kv_buf.shape[2] // ROUNDS // 2

    def kv_rows(part, turn, half):
        first = (turn * 2 + part) * kv_part
        if half is None:
            return pl.ds(first, kv_part)
        return pl.ds(first + half * (kv_part // 2), kv_part // 2)

    def kv_slot(part, turn):
        return lambda c, half: kv_buf.at[core, c, kv_rows(part, turn, half), :]

    def kv_mine(part, turn):
        return lambda half: kv_own.at[kv_rows(part, turn, half), :]

    both = range(2)
    patch = [
        torus_gather(patch_slot(p), own_of(patch_slot(p)), place, p, patch_send, patch_recv)
        for p in both
    ]
    w = [
        [
            torus_gather(w_slot(p, t), own_of(w_slot(p, t)), place, p, w_send, w_recv, t)
            for p in both
        ]
        for t in range(ROUNDS)
    ]
    kv = [
        [
            torus_gather(kv_slot(p, t), kv_mine(p, t), place, p, kv_send, kv_recv, t)
            for p in both
        ]
        for t in range(ROUNDS)
    ]
    rings = {0: 0, -1: 1, 1: 2, 2: 3}

    def cross(turn, part, r, q):
        chip_at = kv[turn][part][3]
        index = rings[r] * 4 + rings[q]
        target = kv_slot(part, turn)(chip_at(r, q), None)
        return pltpu.make_async_remote_copy(
            src_ref=kv_mine(part, turn)(None) if (r, q) == (0, 0) else target,
            dst_ref=target,
            send_sem=pair_send.at[2 * turn + part, index],
            recv_sem=pair_recv.at[2 * turn + part, index],
            device_id={"ctx": sibling}, device_id_type=MESH,
        )

    def ignore(p, r, q):
        pass

    def first(pair):
        for start, *_ in pair:
            start("e0", "e1")
        for start, *_ in pair:
            start(("f0", 0), ("f1", 0))

    def near(pair, also=ignore):
        for p, (start, wait, *_) in enumerate(pair):
            wait("e0")
            start("e2", ("f0", -1), ("f1", -1))
            also(p, -1, 0)
            wait("e1")
            start("e3", ("f0", 1), ("f1", 1))
            also(p, 1, 0)

    def relay(pair, r, also=ignore):
        for p, (start, wait, *_) in enumerate(pair):
            wait(("f0", r))
            start(("f2", r))
            also(p, r, -1)
            wait(("f1", r))
            start(("f3", r))
            also(p, r, 1)

    def far(pair, also=ignore):
        for p, (start, wait, *_) in enumerate(pair):
            wait("e2", "e3")
            start(("f0", 2), ("f1", 2))
            also(p, 2, 0)

    def finish(pair, also=ignore):
        for r in rings:
            for p, (_, wait, *_) in enumerate(pair):
                wait(("f2", r), ("f3", r))
                also(p, r, 2)

    def to_sibling(src, dst, k):
        return pltpu.make_async_remote_copy(
            src_ref=src, dst_ref=dst, send_sem=misc_send.at[k], recv_sem=misc_recv.at[k],
            device_id={"ctx": sibling}, device_id_type=MESH,
        )

    first(patch)

    @pl.when(core == 0)
    def _():
        to_sibling(w_value_ref, w_buf.at[me], 0).start()

    @pl.when(core == 1)
    def _():
        to_sibling(w_key_ref, w_buf.at[me], 0).start()

    text_pair = to_sibling(text_ref, text_buf.at[core], 1)
    text_pair.start()
    choose, pick = frame_places(count_ref[...], offset_ref[...], chip)
    pick_ref[...] = pick

    near(patch)
    w_local(w_key_ref).wait()
    pltpu.make_async_copy(w_buf.at[sibling], w_buf.at[sibling], misc_recv.at[0]).wait()
    for start, *_ in w[0]:
        start("e0", "e1")
    relay(patch, 0)
    far(patch)
    for start, *_ in w[0]:
        start(("f0", 0), ("f1", 0))
    for r in (-1, 1, 2):
        relay(patch, r)
    finish(patch)
    patch_pair = to_sibling(patch_buf.at[core], patch_buf.at[core], 2)
    patch_pair.start()
    near(w[0])
    other = patch_buf.at[1 - core]
    w_merge_in.wait()
    pltpu.make_async_copy(other, other, misc_recv.at[2]).wait()

    group = 4
    per = chips // group

    def merge(i, _):
        rows = patch_buf[i // group, pl.ds(lax.rem(i, group) * per, per)]
        flat = rows.reshape(per * 16, half_in)
        low = jnp.dot(flat, w_merge_ref[:half_in, :], preferred_element_type=jnp.float32)
        high = jnp.dot(flat, w_merge_ref[half_in:, :], preferred_element_type=jnp.float32)
        width = low.shape[1]
        low = low.reshape(per, 16, width)[:, :8]
        high = high.reshape(per, 16, width)[:, 8:]
        merged[pl.ds(pl.multiple_of(i * per * 8, per * 8), per * 8), :] = (
            (low + high).reshape(per * 8, width).astype(jnp.bfloat16)
        )
        return 0

    lax.fori_loop(0, 2 * group, merge, 0)
    chosen = jnp.dot(choose, merged[...], preferred_element_type=jnp.float32)
    rows_out[...] = chosen.astype(jnp.bfloat16).reshape(rows_out.shape)
    rows_in[me] = rows_out[chip]

    def deliver(i, _):
        to = lax.rem(me + i, count)
        pltpu.make_async_remote_copy(
            src_ref=rows_out.at[to // 2], dst_ref=rows_in.at[me],
            send_sem=row_sem.at[0], recv_sem=row_sem.at[1],
            device_id={"ctx": to}, device_id_type=MESH,
        ).start()
        return 0

    lax.fori_loop(1, count, deliver, 0)
    relay(w[0], 0)
    far(w[0])
    relay(w[0], -1)

    depth = iota((HD, span), 0)

    def mark(i, _):
        b = lax.rem(chip + (chips - WINDOW + 1) + i, chips)
        doc = jnp.concatenate([doc_ref[2 * b], doc_ref[2 * b + 1]], axis=1)
        late = jnp.where(b > chip, 1, 0)
        flag = jnp.where(depth < 8, jnp.where(doc != depth, 1, 0), jnp.where(depth == 8, late, 0))
        kx[i] = flag.astype(jnp.float32).astype(jnp.bfloat16)
        return 0

    lax.fori_loop(0, WINDOW, mark, 0)
    side = iota((HD, tok), 0)
    hit = (side == doc_ref[me]) | (side == 8)
    qx[...] = jnp.where(hit, -BIG, 0.0).T.astype(jnp.bfloat16)

    text_own.wait()
    pltpu.make_async_copy(
        text_buf.at[1 - core], text_buf.at[1 - core], misc_recv.at[1]
    ).wait()
    most = rows_in.at[pl.ds(0, count - 1)]
    pltpu.make_async_copy(most, most, row_sem.at[0]).wait()
    pltpu.make_async_copy(most, most, row_sem.at[1]).wait()

    picked = pick_ref[...]
    covered = jnp.sum(picked.astype(jnp.float32), axis=1, keepdims=True) > 0.0

    def join(i, squares):
        placed = jnp.dot(picked, rows_in[i], preferred_element_type=jnp.float32)
        cols = pl.ds(pl.multiple_of(i * chunk, chunk), chunk)
        text = text_buf[:, :, cols].reshape(2 * tok, chunk).astype(jnp.float32)
        value = jnp.where(covered, placed, text)
        joined[i] = value.astype(jnp.bfloat16)
        return squares + value * value

    squares = lax.fori_loop(
        0, count, join, jnp.zeros((2 * tok, chunk), jnp.float32), unroll=2
    )
    mean = jnp.sum(squares, axis=1, keepdims=True) / (count * chunk)
    factor = lax.rsqrt(mean + 1e-06)
    relay(w[0], 1)
    relay(w[0], 2)
    first(w[1])

    def norm(i, _):
        cols = pl.ds(pl.multiple_of(i * chunk, chunk), chunk)
        value = joined[i].astype(jnp.float32)
        normed[i] = (value * factor * gain_ref[:, cols]).astype(jnp.bfloat16)
        return 0

    lax.fori_loop(0, count, norm, 0, unroll=2)

    def project(turn, low, high):
        def add(k, _):
            along = k // 4
            along = lax.rem(jnp.where(along < 2, along, 5 - along), 4)
            across = lax.rem(k, 4)
            one = 2 * (lax.rem(y + along, 4) * 4 + across)
            two = 2 * (across * 4 + lax.rem(x + along, 4)) + 1
            cols = pl.ds(turn * w_cols, w_cols)
            left = jnp.concatenate([normed[one], normed[two]], axis=1)
            right = jnp.concatenate([w_buf[one, :, cols], w_buf[two, :, cols]], axis=0)
            acc[...] += jnp.dot(left, right, preferred_element_type=jnp.float32)
            return 0

        lax.fori_loop(low, high, add, 0)

    def own_block(turn):
        rows = pl.ds(turn * w_cols, w_cols)

        @pl.when(core == 0)
        def _():
            kv_own[rows, :] = acc[...].T.astype(jnp.bfloat16)

        @pl.when(core == 1)
        def _():
            kv_own[rows, :] = acc[...].astype(jnp.bfloat16)

        kv_buf[core, chip, rows, :] = kv_own[rows, :]

    def handed(turn):
        return lambda p, r, q: cross(turn, p, r, q).start()

    def spread(turn):
        first(kv[turn])
        for p in both:
            cross(turn, p, 0, 0).start()

    def arrived(turn):
        for part in both:
            for r in rings:
                for q in rings:
                    rows = kv_rows(part, turn, None)
                    block = kv_buf.at[1 - core, kv[turn][part][3](r, q), rows, :]
                    index = rings[r] * 4 + rings[q]
                    pltpu.make_async_copy(
                        block, block, pair_recv.at[2 * turn + part, index]
                    ).wait()

    acc[...] = jnp.zeros_like(acc)
    project(0, 0, 12)
    finish(w[0])
    project(0, 12, 16)
    own_block(0)
    spread(0)
    near(kv[0], handed(0))
    near(w[1])
    relay(kv[0], 0, handed(0))
    far(kv[0], handed(0))
    for r in (-1, 1, 2):
        relay(kv[0], r, handed(0))
    relay(w[1], 0)
    far(w[1])
    finish(kv[0], handed(0))
    arrived(0)
    query_in.wait()

    width = CHUNK_HEADS * HD
    chunks = q_ref.shape[1] // width
    middle = chunks // 2
    per_kv = 16 // CHUNK_HEADS
    rate = math.log2(math.e) / math.sqrt(HD)

    def hop(c):
        return pltpu.make_async_remote_copy(
            src_ref=stage.at[c], dst_ref=landed.at[c],
            send_sem=hop_send.at[c], recv_sem=hop_recv.at[c],
            device_id={"section": after}, device_id_type=MESH,
        )

    def chain(c):
        cols = pl.ds(pl.multiple_of(c * width, width), width)

        @pl.when(section == 0)
        def _():
            rows = pl.ds(pl.multiple_of(core * tok, tok), tok)
            hidden[...] = jnp.concatenate(
                [joined[2 * c, rows, :], joined[2 * c + 1, rows, :]], axis=1
            )

        @pl.when(section > 0)
        def _():
            hop(c).wait_recv()
            hidden[...] = landed[c]

        fresh = (hidden[...].astype(jnp.float32) + mixed[c]).astype(jnp.bfloat16)
        out_ref[:, cols] = fresh

        @pl.when(section < sections - 1)
        def _():
            stage[c] = fresh
            hop(c).start()

    def attend(i):
        head = i // per_kv
        kcols = pl.ds(pl.multiple_of(head * HD, HD), HD)
        vrows = pl.ds(pl.multiple_of(head // 2 * span, span), span)
        vcols = pl.ds(pl.multiple_of(lax.rem(head, 2) * HD, HD), HD)
        where = [lax.rem(chip + (chips - WINDOW + 1) + b, chips) for b in range(WINDOW)]
        kc = [
            jnp.concatenate([kv_buf[0, b, kcols, :], kx[n]], axis=0) for n, b in enumerate(where)
        ]
        ones = jnp.ones((span, HD), jnp.bfloat16)
        vc = [jnp.concatenate([kv_buf[1, b, vrows, vcols], ones], axis=1) for b in where]
        kc = jnp.concatenate(kc, axis=1)
        vc = jnp.concatenate(vc, axis=0)
        last = (WINDOW - 1) * span
        row = iota((tok, span), 0) + core * tok
        col = iota((tok, span), 1)
        for h in range(CHUNK_HEADS):
            qh = q_ref[:, pl.ds(pl.multiple_of(i * width, width) + h * HD, HD)]
            qc = jnp.concatenate([qh, qx[...]], axis=1)
            s = jnp.dot(qc, kc, preferred_element_type=jnp.float32)
            own = jnp.where(col <= row, s[:, last:], -BIG)
            s = jnp.concatenate([s[:, :last], own], axis=1)
            top = jnp.max(s, axis=1, keepdims=True)
            p = jnp.exp2((s - top) * rate).astype(jnp.bfloat16)
            r = jnp.dot(p, vc, preferred_element_type=jnp.float32)
            mixed[i, :, h * HD : (h + 1) * HD] = r[:, :HD] / r[:, HD:]

    def step(i, _):
        attend(i)
        c = i - section

        @pl.when(((i < middle) & (c >= 0)) | (c >= middle))
        def _():
            chain(c)

        @pl.when(i == 0)
        def _():
            relay(w[1], -1)

        @pl.when(i == 1)
        def _():
            relay(w[1], 1)

        @pl.when(i == 2)
        def _():
            relay(w[1], 2)

        @pl.when(i == 3)
        def _():
            acc[...] = jnp.zeros_like(acc)
            project(1, 0, 12)
            finish(w[1])
            project(1, 12, 16)
            own_block(1)
            spread(1)

        @pl.when(i == 4)
        def _():
            near(kv[1], handed(1))

        @pl.when(i == 5)
        def _():
            relay(kv[1], 0, handed(1))
            far(kv[1], handed(1))

        @pl.when(i == 6)
        def _():
            for r in (-1, 1, 2):
                relay(kv[1], r, handed(1))

        @pl.when(i == middle - 1)
        def _():
            finish(kv[1], handed(1))

            def catch_up(d, _):
                chain(middle - section + d)
                return 0

            lax.fori_loop(0, section, catch_up, 0)
            arrived(1)

        return 0

    lax.fori_loop(0, chunks, step, 0)

    def tail(d, _):
        chain(chunks - section + d)
        return 0

    lax.fori_loop(0, section, tail, 0)

    @pl.when(section < sections - 1)
    def _():
        def drain(c, _):
            hop(c).wait_send()
            return 0

        lax.fori_loop(0, chunks, drain, 0)

    for turn in range(ROUNDS):
        for part in both:
            for r in rings:
                for q in rings:
                    cross(turn, part, r, q).wait_send()
    for gather in (patch, *w, *kv):
        for _, _, drain, _ in gather:
            drain()
    to_sibling(w_value_ref, w_buf.at[me], 0).wait_send()
    text_pair.wait_send()
    patch_pair.wait_send()


def window(patches, vis_gain, w_merge, counts, offsets, docs, text, gain, w_key, w_value, query):
    count = lax.axis_size("ctx")
    tok, width = text.shape
    chunk = width // count
    kv_width = w_key.shape[1]
    chips = count // 2
    cols = CHUNK_HEADS * HD
    chunks = width // cols
    bf16, f32 = jnp.bfloat16, jnp.float32
    vmem = pl.BlockSpec(memory_space=pltpu.VMEM)
    hbm = pl.BlockSpec(memory_space=pl.ANY)
    dma = pltpu.SemaphoreType.DMA
    return pl.pallas_call(
        window_kernel,
        out_shape=jax.ShapeDtypeStruct((tok, width), bf16),
        in_specs=[vmem, vmem, hbm, vmem, vmem, vmem, hbm, vmem, hbm, hbm, hbm],
        out_specs=vmem,
        scratch_shapes=[
            pltpu.VMEM((2, chips, 16, patches.shape[1] // 2), bf16),
            pltpu.VMEM(w_merge.shape, bf16),
            pltpu.VMEM((count * 8, chunk), bf16),
            pltpu.VMEM((chips, 32, chunk), bf16),
            pltpu.VMEM((count, 32, chunk), bf16),
            pltpu.VMEM((2, tok, width), bf16),
            pltpu.VMEM((count, 2 * tok, chunk), bf16),
            pltpu.VMEM((count, 2 * tok, chunk), bf16),
            pltpu.VMEM((count, chunk, kv_width), bf16),
            pltpu.VMEM((2 * tok, kv_width // ROUNDS), f32),
            pltpu.VMEM((kv_width, 2 * tok), bf16),
            pltpu.VMEM((2, chips, kv_width, 2 * tok), bf16),
            pltpu.VMEM((tok, width), bf16),
            pltpu.VMEM((2 * tok, 32), bf16),
            pltpu.VMEM((WINDOW, HD, 2 * tok), bf16),
            pltpu.VMEM((tok, HD), bf16),
            pltpu.VMEM((chunks, tok, cols), f32),
            pltpu.VMEM((tok, cols), bf16),
            pltpu.VMEM((chunks, tok, cols), bf16),
            pltpu.VMEM((chunks, tok, cols), bf16),
        ]
        + [dma((2, 20))] * 2
        + [dma((2 * ROUNDS, 20))] * 4
        + [dma((2 * ROUNDS, 16))] * 2
        + [dma((2,)), dma((3,)), dma((3,)), dma((4,)), dma((chunks,)), dma((chunks,))],
        compiler_params=pltpu.CompilerParams(
            collective_id=1, has_side_effects=True, vmem_limit_bytes=60 * 2**20
        ),
        cost_estimate=pl.CostEstimate(
            flops=24 * 10**9, bytes_accessed=12 * 2**20, transcendentals=tok * 64 * 2304
        ),
    )(patches, vis_gain, w_merge, counts, offsets, docs, text, gain, w_key, w_value, query)


def shards(
    text_embeds,
    patches,
    vis_gain,
    w_merge,
    frame_count,
    frame_offset,
    doc_ids,
    norm_gain,
    w_key,
    w_value,
    queries,
):
    count = lax.axis_size("ctx")
    result = window(
        patches,
        vis_gain[None],
        w_merge,
        frame_count[None],
        frame_offset[None],
        doc_ids.reshape(count, 1, -1),
        text_embeds,
        norm_gain,
        w_key[0],
        w_value[0],
        queries[0],
    )
    return result[None]


def solution(mesh):
    return jax.shard_map(
        shards,
        mesh=mesh,
        in_specs=(
            P("ctx", None),
            P("ctx", None),
            P(),
            P(None, "ctx"),
            P(),
            P(),
            P(),
            P("section", None),
            P("section", "ctx", None),
            P("section", "ctx", None),
            P("section", "ctx", None),
        ),
        out_specs=P("section", "ctx", None),
        check_vma=False,
    )
```

time: 390 us -> 153 us (0.39)
  waiting for transfers between devices: 251 us -> 0 us
  Pallas kernels: 64.9 us -> 149 us
  other arithmetic: 25.8 us -> 0 us
  matrix products: 20.5 us -> 0 us
  between operations: 13.6 us -> 0.01 us
  local copies, waits for them, and re-layouts: 12.9 us -> 3.1 us
    all_gather x6 -> x0, waiting for transfers between devices: 249 us -> none  [the longest x1 49.4 us: shards(): lax.all_gather(w_key[0], 'ctx', axis=0, tiled=True)]
    pallas_call x1, Pallas kernels: 64.9 us -> 149 us  [window(): pl.pallas_call(window_kernel, out_shape=jax.ShapeDtypeStruct((tok, width)...]
    dot_general x4 -> x0, matrix products: 20.5 us -> none  [the longest x1 5.98 us: shards(): value_sum = jnp.dot(normed, pieces[1], preferred_element_type=jnp.float32)]
    lt x2 -> x0, other arithmetic: 15.7 us -> none  [the longest x1 15.7 us: shards(): used = slot % slot_dev < frame_count[owner]]
    reshape x1 -> x0, local copies, waits for them, and re-layouts: 6.39 us -> none  [shards(): keys_t = all_keys.reshape(chips, 2 * tok_count, kv_width).transpose(0, 2, 1)]
    gather x27 -> x0, other arithmetic: 5.46 us -> none  [the longest x26 5.45 us: shards(): used = slot % slot_dev < frame_count[owner]]
  transfers between devices with their start and end apart: 6 -> 0, of which waited for: 6 -> 0; matrix products, arithmetic and copies ran while one was open for 13% -> 0% of each run, Pallas kernels for 0% -> 0%
where the time goes in v3:
time: 153 us; the launch traced here: 152 us
  Pallas kernels  149 us (97%)
  local copies, waits for them, and re-layouts  3.1 us (2%)
    pallas_call x1, Pallas kernels, window(): pl.pallas_call(window_kernel, out_shape=jax.ShapeDtypeStruct((tok, width)...  149 us
    unnamed x1, local copies, waits for them, and re-layouts  3.1 us

profile of v3, /device:TPU:96, one launch (start us, length us, event | category | flops | bytes accessed | tf_op | source)
XLA Modules:
  0.0 152.3 jit_solution(17917840497763426045)
XLA Ops:
  0.0 149.2 %shard_map.109 = bf16[128,8192]{1,0:T(8,128)(2,1)} custom-call(bf16[8,5120]{1,0:T(8,128)(2,1)} %patches_ref.1, f32[1,5120]{1,0:T(1,128)} %bitcast.12, bf16[5120,256]{1,0:T(8,128)(2,1)} %w_merge_hbm.1, s32[1,32]{1,0:T(1,128)} %bitcast.14, s32[1,64]{1,0:T(1,128)} %bitcast.15, s32[32,1,128]{2,1,0:T(1,128)} %bitcast.13, bf16[128,8192]{1,0:T(8,128)(2,1)} %text_ref.1, ...), custom_call_target="tpu_custom_call" | custom-call | flops 24000000000 | bytes 12582912 | tf_op jit(solution)/shard_map/pallas_call | solution.py:639
  149.2 3.1 %copy.13 = bf16[1,128,8192]{2,1,0:T(8,128)(2,1)} copy(bf16[1,128,8192]{2,1,0:T(8,128)(2,1)} %bitcast.8) | data formatting | bytes 4194304

commit v4 on v3

--- a/solution.py
+++ b/solution.py
@@ -135,12 +135,12 @@
     barrier = pltpu.get_barrier_semaphore()
 
     def greet(i, _):
-        pl.semaphore_signal(
-            barrier, inc=1, device_id={"ctx": lax.rem(me + i, count)}, device_id_type=MESH
-        )
+        peer = lax.rem(chip + i, chips) * 2 + core
+        pl.semaphore_signal(barrier, inc=1, device_id={"ctx": peer}, device_id_type=MESH)
         return 0
 
-    lax.fori_loop(1, count, greet, 0)
+    lax.fori_loop(1, chips, greet, 0)
+    pl.semaphore_signal(barrier, inc=1, device_id={"ctx": sibling}, device_id_type=MESH)
     before = lax.rem(section + sections - 1, sections)
     after = lax.rem(section + 1, sections)
     pl.semaphore_signal(barrier, inc=1, device_id={"section": before}, device_id_type=MESH)
@@ -172,7 +172,7 @@
         [wide[:, :half_in], wide[:, half_in:]], axis=0
     ).astype(jnp.bfloat16)
 
-    pl.semaphore_wait(barrier, count)
+    pl.semaphore_wait(barrier, chips + 1)
 
     def patch_slot(part):
         def at(c, half):
@@ -321,41 +321,43 @@
     patch_pair = to_sibling(patch_buf.at[core], patch_buf.at[core], 2)
     patch_pair.start()
     near(w[0])
-    other = patch_buf.at[1 - core]
-    w_merge_in.wait()
-    pltpu.make_async_copy(other, other, misc_recv.at[2]).wait()
-
-    group = 4
-    per = chips // group
-
-    def merge(i, _):
-        rows = patch_buf[i // group, pl.ds(lax.rem(i, group) * per, per)]
-        flat = rows.reshape(per * 16, half_in)
+    def merge(q):
+        flat = patch_buf[q].reshape(chips * 16, half_in)
         low = jnp.dot(flat, w_merge_ref[:half_in, :], preferred_element_type=jnp.float32)
         high = jnp.dot(flat, w_merge_ref[half_in:, :], preferred_element_type=jnp.float32)
         width = low.shape[1]
-        low = low.reshape(per, 16, width)[:, :8]
-        high = high.reshape(per, 16, width)[:, 8:]
-        merged[pl.ds(pl.multiple_of(i * per * 8, per * 8), per * 8), :] = (
-            (low + high).reshape(per * 8, width).astype(jnp.bfloat16)
+        low = low.reshape(chips, 16, width)[:, :8]
+        high = high.reshape(chips, 16, width)[:, 8:]
+        merged[pl.ds(pl.multiple_of(q * chips * 8, chips * 8), chips * 8), :] = (
+            (low + high).reshape(chips * 8, width).astype(jnp.bfloat16)
         )
+
+    w_merge_in.wait()
+
+    def merge_step(i, _):
+        @pl.when(i == 1)
+        def _():
+            other = patch_buf.at[1 - core]
+            pltpu.make_async_copy(other, other, misc_recv.at[2]).wait()
+
+        merge(lax.rem(core + i, 2))
         return 0
 
-    lax.fori_loop(0, 2 * group, merge, 0)
+    lax.fori_loop(0, 2, merge_step, 0)
     chosen = jnp.dot(choose, merged[...], preferred_element_type=jnp.float32)
     rows_out[...] = chosen.astype(jnp.bfloat16).reshape(rows_out.shape)
-    rows_in[me] = rows_out[chip]
+    rows_in[core, chip] = rows_out[chip]
 
     def deliver(i, _):
-        to = lax.rem(me + i, count)
+        to = lax.rem(chip + i, chips)
         pltpu.make_async_remote_copy(
-            src_ref=rows_out.at[to // 2], dst_ref=rows_in.at[me],
+            src_ref=rows_out.at[to], dst_ref=rows_in.at[core, chip],
             send_sem=row_sem.at[0], recv_sem=row_sem.at[1],
-            device_id={"ctx": to}, device_id_type=MESH,
+            device_id={"ctx": to * 2 + core}, device_id_type=MESH,
         ).start()
         return 0
 
-    lax.fori_loop(1, count, deliver, 0)
+    lax.fori_loop(1, chips, deliver, 0)
     relay(w[0], 0)
     far(w[0])
     relay(w[0], -1)
@@ -375,19 +377,26 @@
     hit = (side == doc_ref[me]) | (side == 8)
     qx[...] = jnp.where(hit, -BIG, 0.0).T.astype(jnp.bfloat16)
 
+    most = rows_in.at[core, pl.ds(0, chips - 1)]
+    pltpu.make_async_copy(most, most, row_sem.at[1]).wait()
+    row_pair = to_sibling(rows_in.at[core], rows_in.at[core], 3)
+    row_pair.start()
+    pltpu.make_async_copy(most, most, row_sem.at[0]).wait()
+    relay(w[0], 1)
+    relay(w[0], 2)
+    first(w[1])
     text_own.wait()
     pltpu.make_async_copy(
         text_buf.at[1 - core], text_buf.at[1 - core], misc_recv.at[1]
     ).wait()
-    most = rows_in.at[pl.ds(0, count - 1)]
-    pltpu.make_async_copy(most, most, row_sem.at[0]).wait()
-    pltpu.make_async_copy(most, most, row_sem.at[1]).wait()
+    rest = rows_in.at[1 - core]
+    pltpu.make_async_copy(rest, rest, misc_recv.at[3]).wait()
 
     picked = pick_ref[...]
     covered = jnp.sum(picked.astype(jnp.float32), axis=1, keepdims=True) > 0.0
 
     def join(i, squares):
-        placed = jnp.dot(picked, rows_in[i], preferred_element_type=jnp.float32)
+        placed = jnp.dot(picked, rows_in[lax.rem(i, 2), i // 2], preferred_element_type=jnp.float32)
         cols = pl.ds(pl.multiple_of(i * chunk, chunk), chunk)
         text = text_buf[:, :, cols].reshape(2 * tok, chunk).astype(jnp.float32)
         value = jnp.where(covered, placed, text)
@@ -395,36 +404,31 @@
         return squares + value * value
 
     squares = lax.fori_loop(
-        0, count, join, jnp.zeros((2 * tok, chunk), jnp.float32), unroll=2
+        0, count, join, jnp.zeros((2 * tok, chunk), jnp.float32), unroll=4
     )
     mean = jnp.sum(squares, axis=1, keepdims=True) / (count * chunk)
     factor = lax.rsqrt(mean + 1e-06)
-    relay(w[0], 1)
-    relay(w[0], 2)
-    first(w[1])
 
     def norm(i, _):
         cols = pl.ds(pl.multiple_of(i * chunk, chunk), chunk)
         value = joined[i].astype(jnp.float32)
-        normed[i] = (value * factor * gain_ref[:, cols]).astype(jnp.bfloat16)
+        normed[:, cols] = (value * factor * gain_ref[:, cols]).astype(jnp.bfloat16)
         return 0
 
-    lax.fori_loop(0, count, norm, 0, unroll=2)
-
-    def project(turn, low, high):
+    lax.fori_loop(0, count, norm, 0, unroll=4)
+
+    def project(turn):
+        cols = pl.ds(turn * w_cols, w_cols)
+        deep = 8
+
         def add(k, _):
-            along = k // 4
-            along = lax.rem(jnp.where(along < 2, along, 5 - along), 4)
-            across = lax.rem(k, 4)
-            one = 2 * (lax.rem(y + along, 4) * 4 + across)
-            two = 2 * (across * 4 + lax.rem(x + along, 4)) + 1
-            cols = pl.ds(turn * w_cols, w_cols)
-            left = jnp.concatenate([normed[one], normed[two]], axis=1)
-            right = jnp.concatenate([w_buf[one, :, cols], w_buf[two, :, cols]], axis=0)
-            acc[...] += jnp.dot(left, right, preferred_element_type=jnp.float32)
+            lanes = pl.ds(pl.multiple_of(k * deep * chunk, deep * chunk), deep * chunk)
+            right = w_buf[pl.ds(k * deep, deep), :, cols].reshape(deep * chunk, w_cols)
+            acc[...] += jnp.dot(normed[:, lanes], right, preferred_element_type=jnp.float32)
             return 0
 
-        lax.fori_loop(low, high, add, 0)
+        acc[...] = jnp.zeros_like(acc)
+        lax.fori_loop(0, count // deep, add, 0)
 
     def own_block(turn):
         rows = pl.ds(turn * w_cols, w_cols)
@@ -458,10 +462,8 @@
                         block, block, pair_recv.at[2 * turn + part, index]
                     ).wait()
 
-    acc[...] = jnp.zeros_like(acc)
-    project(0, 0, 12)
     finish(w[0])
-    project(0, 12, 16)
+    project(0)
     own_block(0)
     spread(0)
     near(kv[0], handed(0))
@@ -472,9 +474,16 @@
         relay(kv[0], r, handed(0))
     relay(w[1], 0)
     far(w[1])
+    relay(w[1], -1)
     finish(kv[0], handed(0))
     arrived(0)
     query_in.wait()
+
+    def sent(turn):
+        for part in both:
+            for r in rings:
+                for q in rings:
+                    cross(turn, part, r, q).wait_send()
 
     width = CHUNK_HEADS * HD
     chunks = q_ref.shape[1] // width
@@ -549,38 +558,36 @@
 
         @pl.when(i == 0)
         def _():
-            relay(w[1], -1)
+            relay(w[1], 1)
 
         @pl.when(i == 1)
         def _():
-            relay(w[1], 1)
+            relay(w[1], 2)
 
         @pl.when(i == 2)
         def _():
-            relay(w[1], 2)
-
-        @pl.when(i == 3)
-        def _():
-            acc[...] = jnp.zeros_like(acc)
-            project(1, 0, 12)
             finish(w[1])
-            project(1, 12, 16)
+            project(1)
             own_block(1)
             spread(1)
 
+        @pl.when(i == 3)
+        def _():
+            near(kv[1], handed(1))
+
         @pl.when(i == 4)
-        def _():
-            near(kv[1], handed(1))
-
-        @pl.when(i == 5)
         def _():
             relay(kv[1], 0, handed(1))
             far(kv[1], handed(1))
 
+        @pl.when(i == 5)
+        def _():
+            relay(kv[1], -1, handed(1))
+            relay(kv[1], 1, handed(1))
+
         @pl.when(i == 6)
         def _():
-            for r in (-1, 1, 2):
-                relay(kv[1], r, handed(1))
+            relay(kv[1], 2, handed(1))
 
         @pl.when(i == middle - 1)
         def _():
@@ -592,6 +599,31 @@
 
             lax.fori_loop(0, section, catch_up, 0)
             arrived(1)
+
+        @pl.when(i == middle)
+        def _():
+            for gather in (patch, w[0]):
+                for _, _, drain, _ in gather:
+                    drain()
+
+        @pl.when(i == middle + 1)
+        def _():
+            for gather in (w[1], kv[0]):
+                for _, _, drain, _ in gather:
+                    drain()
+
+        @pl.when(i == middle + 2)
+        def _():
+            sent(0)
+
+        @pl.when(i == middle + 3)
+        def _():
+            sent(1)
+
+        @pl.when(i == middle + 4)
+        def _():
+            for _, _, drain, _ in kv[1]:
+                drain()
 
         return 0
 
@@ -611,17 +643,10 @@
 
         lax.fori_loop(0, chunks, drain, 0)
 
-    for turn in range(ROUNDS):
-        for part in both:
-            for r in rings:
-                for q in rings:
-                    cross(turn, part, r, q).wait_send()
-    for gather in (patch, *w, *kv):
-        for _, _, drain, _ in gather:
-            drain()
     to_sibling(w_value_ref, w_buf.at[me], 0).wait_send()
     text_pair.wait_send()
     patch_pair.wait_send()
+    row_pair.wait_send()
 
 
 def window(patches, vis_gain, w_merge, counts, offsets, docs, text, gain, w_key, w_value, query):
@@ -646,10 +671,10 @@
             pltpu.VMEM(w_merge.shape, bf16),
             pltpu.VMEM((count * 8, chunk), bf16),
             pltpu.VMEM((chips, 32, chunk), bf16),
-            pltpu.VMEM((count, 32, chunk), bf16),
+            pltpu.VMEM((2, chips, 32, chunk), bf16),
             pltpu.VMEM((2, tok, width), bf16),
             pltpu.VMEM((count, 2 * tok, chunk), bf16),
-            pltpu.VMEM((count, 2 * tok, chunk), bf16),
+            pltpu.VMEM((2 * tok, width), bf16),
             pltpu.VMEM((count, chunk, kv_width), bf16),
             pltpu.VMEM((2 * tok, kv_width // ROUNDS), f32),
             pltpu.VMEM((kv_width, 2 * tok), bf16),
@@ -666,7 +691,7 @@
         + [dma((2, 20))] * 2
         + [dma((2 * ROUNDS, 20))] * 4
         + [dma((2 * ROUNDS, 16))] * 2
-        + [dma((2,)), dma((3,)), dma((3,)), dma((4,)), dma((chunks,)), dma((chunks,))],
+        + [dma((2,)), dma((4,)), dma((4,)), dma((4,)), dma((chunks,)), dma((chunks,))],
         compiler_params=pltpu.CompilerParams(
             collective_id=1, has_side_effects=True, vmem_limit_bytes=60 * 2**20
         ),

time: 153 us -> 143 us (0.935)
  Pallas kernels: 149 us -> 140 us
    pallas_call x1, Pallas kernels: 149 us -> 140 us  [window(): pl.pallas_call(window_kernel, out_shape=jax.ShapeDtypeStruct((tok, width)...]
where the time goes in v4:
time: 143 us
  Pallas kernels  140 us (98%)
  local copies, waits for them, and re-layouts  3.1 us (2%)
    pallas_call x1, Pallas kernels, window(): pl.pallas_call(window_kernel, out_shape=jax.ShapeDtypeStruct((tok, width)...  140 us
    unnamed x1, local copies, waits for them, and re-layouts  3.1 us

profile of v4, /device:TPU:96, one launch (start us, length us, event | category | flops | bytes accessed | tf_op | source)
XLA Modules:
  0.0 143.0 jit_solution(16728587227450234761)
XLA Ops:
  0.0 139.9 %shard_map.109 = bf16[128,8192]{1,0:T(8,128)(2,1)} custom-call(bf16[8,5120]{1,0:T(8,128)(2,1)} %patches_ref.1, f32[1,5120]{1,0:T(1,128)} %bitcast.12, bf16[5120,256]{1,0:T(8,128)(2,1)} %w_merge_hbm.1, s32[1,32]{1,0:T(1,128)} %bitcast.14, s32[1,64]{1,0:T(1,128)} %bitcast.15, s32[32,1,128]{2,1,0:T(1,128)} %bitcast.13, bf16[128,8192]{1,0:T(8,128)(2,1)} %text_ref.1, ...), custom_call_target="tpu_custom_call" | custom-call | flops 24000000000 | bytes 12582912 | tf_op jit(solution)/shard_map/pallas_call | solution.py:664
  139.9 3.1 %copy.13 = bf16[1,128,8192]{2,1,0:T(8,128)(2,1)} copy(bf16[1,128,8192]{2,1,0:T(8,128)(2,1)} %bitcast.8) | data formatting | bytes 4194304

commit v5 on v4

--- a/solution.py
+++ b/solution.py
@@ -384,7 +384,6 @@
     pltpu.make_async_copy(most, most, row_sem.at[0]).wait()
     relay(w[0], 1)
     relay(w[0], 2)
-    first(w[1])
     text_own.wait()
     pltpu.make_async_copy(
         text_buf.at[1 - core], text_buf.at[1 - core], misc_recv.at[1]
@@ -466,6 +465,7 @@
     project(0)
     own_block(0)
     spread(0)
+    first(w[1])
     near(kv[0], handed(0))
     near(w[1])
     relay(kv[0], 0, handed(0))

time: 143 us -> 147 us (1.028)
  Pallas kernels: 140 us -> 144 us
    pallas_call x1, Pallas kernels: 140 us -> 144 us  [window(): pl.pallas_call(window_kernel, out_shape=jax.ShapeDtypeStruct((tok, width)...]
where the time goes in v5:
time: 147 us
  Pallas kernels  144 us (98%)
  local copies, waits for them, and re-layouts  3.1 us (2%)
    pallas_call x1, Pallas kernels, window(): pl.pallas_call(window_kernel, out_shape=jax.ShapeDtypeStruct((tok, width)...  144 us
    unnamed x1, local copies, waits for them, and re-layouts  3.1 us

profile of v5, /device:TPU:96, one launch (start us, length us, event | category | flops | bytes accessed | tf_op | source)
XLA Modules:
  0.0 147.0 jit_solution(5272176735574943636)
XLA Ops:
  0.0 143.9 %shard_map.109 = bf16[128,8192]{1,0:T(8,128)(2,1)} custom-call(bf16[8,5120]{1,0:T(8,128)(2,1)} %patches_ref.1, f32[1,5120]{1,0:T(1,128)} %bitcast.12, bf16[5120,256]{1,0:T(8,128)(2,1)} %w_merge_hbm.1, s32[1,32]{1,0:T(1,128)} %bitcast.14, s32[1,64]{1,0:T(1,128)} %bitcast.15, s32[32,1,128]{2,1,0:T(1,128)} %bitcast.13, bf16[128,8192]{1,0:T(8,128)(2,1)} %text_ref.1, ...), custom_call_target="tpu_custom_call" | custom-call | flops 24000000000 | bytes 12582912 | tf_op jit(solution)/shard_map/pallas_call | solution.py:664
  143.9 3.1 %copy.13 = bf16[1,128,8192]{2,1,0:T(8,128)(2,1)} copy(bf16[1,128,8192]{2,1,0:T(8,128)(2,1)} %bitcast.8) | data formatting | bytes 4194304
